TPU v7x, 32 devices: a whole 2x2x4 slice. The times are simulated.
32 devices in a mesh: dp: 8 (over y, x, core), mp: 4 (over z).
Axes of the slice: x: 2, y: 2, z: 4, core: 2. Of those that a mesh axis runs over, the one named last changes fastest.
Arguments:
- ids: int32 [32768], P('dp'), may hold values from 0 to 32767
- hash_mult: int32 [1024], replicated, may hold values from 1 to 65520
- hash_add: int32 [1024], replicated, may hold values from 0 to 65520
- weight_first: bfloat16 [1800, 1024], P('mp'), may hold values from -0.1875 to 0.1875
- bias_first: float32 [1800], P('mp'), may hold values from -4 to 4
- scale_first: float32 [1800], P('mp'), may hold values from 0.1 to 1.9
- shift_first: float32 [1800], P('mp'), may hold values from -3 to 3
- weight_second: bfloat16 [1800, 1800], P('mp'), may hold values from -0.125 to 0.125
- bias_second: float32 [1800], P('mp'), may hold values from -4 to 4
- scale_second: float32 [1800], P('mp'), may hold values from 0.1 to 1.9
- shift_second: float32 [1800], P('mp'), may hold values from -3 to 3
- cotangent: bfloat16 [1800, 32768], P('mp', 'dp'), may hold values from -6 to 6
Outputs:
- output: bfloat16 [1800, 32768], P('mp', 'dp')
- grad_weight_first: float32 [1800, 1024], P('mp')
- grad_bias_first: float32 [1800], P('mp')
- grad_scale_first: float32 [1800], P('mp')
- grad_shift_first: float32 [1800], P('mp')
- grad_weight_second: float32 [1800, 1800], P('mp')
- grad_bias_second: float32 [1800], P('mp')
- grad_scale_second: float32 [1800], P('mp')
- grad_shift_second: float32 [1800], P('mp')
All inputs are finite; a program needn't handle non-finite values.
Results may differ from a plain program's by a relative error of at most 0.03.
Values may be sent and summed in bfloat16 or wider, within the bound.
A program may use at most 192 MiB of HBM per device.

v0:
```python
import jax
import jax.numpy as jnp
from jax import lax
from jax.sharding import PartitionSpec as P

epsilon = 1e-05


def mish_parts(value):
    soft = jnp.tanh(jax.nn.softplus(value))
    slope = soft + value * (1.0 - soft * soft) * jax.nn.sigmoid(value)
    return (value * soft, slope)


def norm_back(grad_out, normed, scale, inv_std, sums, total):
    shift_grad, scale_grad = sums
    return (
        scale[:, None]
        * inv_std
        * (grad_out - shift_grad[:, None] / total - normed * scale_grad[:, None] / total)
    )


def per_device(
    ids,
    hash_mult,
    hash_add,
    weight_first,
    bias_first,
    scale_first,
    shift_first,
    weight_second,
    bias_second,
    scale_second,
    shift_second,
    cotangent,
):
    total = ids.shape[0] * lax.axis_size("dp")
    hashed = (ids[:, None] * hash_mult[None, :] + hash_add[None, :]) % 65521
    encoding = (hashed.astype(jnp.float32) * (2.0 / 65520.0) - 1.0).astype(jnp.bfloat16)
    pre_first = (
        lax.dot_general(
            weight_first, encoding, (((1,), (1,)), ((), ())), preferred_element_type=jnp.float32
        )
        + bias_first[:, None]
    )
    act_first, slope_first = mish_parts(pre_first)
    sum_first, square_first = lax.psum(
        (jnp.sum(act_first, 1), jnp.sum(act_first * act_first, 1)), "dp"
    )
    mean_first = (sum_first / total)[:, None]
    inv_first = lax.rsqrt(square_first[:, None] / total - mean_first * mean_first + epsilon)
    norm_first = (act_first - mean_first) * inv_first
    hidden = (norm_first * scale_first[:, None] + shift_first[:, None]).astype(jnp.bfloat16)
    column_block = lax.all_to_all(weight_second, "mp", split_axis=1, concat_axis=0, tiled=True)
    pre_second = (
        lax.dot_general(
            column_block,
            lax.all_gather(hidden, "mp", axis=0, tiled=True),
            (((0,), (0,)), ((), ())),
            preferred_element_type=jnp.float32,
        )
        + bias_second[:, None]
    )
    act_second, slope_second = mish_parts(pre_second)
    sum_second, square_second = lax.psum(
        (jnp.sum(act_second, 1), jnp.sum(act_second * act_second, 1)), "dp"
    )
    mean_second = (sum_second / total)[:, None]
    inv_second = lax.rsqrt(square_second[:, None] / total - mean_second * mean_second + epsilon)
    norm_second = (act_second - mean_second) * inv_second
    output = (norm_second * scale_second[:, None] + shift_second[:, None]).astype(jnp.bfloat16)
    grad_out = cotangent.astype(jnp.float32)
    sums_second = lax.psum((jnp.sum(grad_out, 1), jnp.sum(grad_out * norm_second, 1)), "dp")
    d_act_second = norm_back(grad_out, norm_second, scale_second, inv_second, sums_second, total)
    d_pre_second = (d_act_second * slope_second).astype(jnp.bfloat16)
    grad_bias_second = jnp.sum(d_pre_second.astype(jnp.float32), 1)
    piece = lax.all_gather(d_pre_second, "mp", axis=0, tiled=True)
    d_hidden = jnp.dot(weight_second, piece, preferred_element_type=jnp.float32)
    block = lax.dot_general(
        hidden, piece, (((1,), (1,)), ((), ())), preferred_element_type=jnp.float32
    )
    d_hidden, local_weight_second = (d_hidden, block)
    grad_weight_second, grad_bias_second = (
        lax.psum(local_weight_second.astype(jnp.bfloat16), "dp").astype(jnp.float32),
        lax.psum(grad_bias_second.astype(jnp.bfloat16), "dp").astype(jnp.float32),
    )
    sums_first = lax.psum((jnp.sum(d_hidden, 1), jnp.sum(d_hidden * norm_first, 1)), "dp")
    d_act_first = norm_back(d_hidden, norm_first, scale_first, inv_first, sums_first, total)
    d_pre_first = (d_act_first * slope_first).astype(jnp.bfloat16)
    local_bias_first = jnp.sum(d_pre_first.astype(jnp.float32), 1)
    local_weight_first = jnp.dot(d_pre_first, encoding, preferred_element_type=jnp.float32)
    grad_weight_first, grad_bias_first = (
        lax.psum(local_weight_first.astype(jnp.bfloat16), "dp").astype(jnp.float32),
        lax.psum(local_bias_first.astype(jnp.bfloat16), "dp").astype(jnp.float32),
    )
    return (
        output,
        grad_weight_first,
        grad_bias_first,
        sums_first[1],
        sums_first[0],
        grad_weight_second,
        grad_bias_second,
        sums_second[1],
        sums_second[0],
    )


def solution(mesh):
    return jax.shard_map(
        per_device,
        mesh=mesh,
        in_specs=(
            P("dp"),
            P(),
            P(),
            P("mp", None),
            P("mp"),
            P("mp"),
            P("mp"),
            P("mp", None),
            P("mp"),
            P("mp"),
            P("mp"),
            P("mp", "dp"),
        ),
        out_specs=(
            P("mp", "dp"),
            P("mp", None),
            P("mp"),
            P("mp"),
            P("mp"),
            P("mp", None),
            P("mp"),
            P("mp"),
            P("mp"),
        ),
        check_vma=False,
    )
```

profile of v0, /device:TPU:9, one launch (start us, length us, event | category | flops | bytes accessed | tf_op | source)
XLA Modules:
  0.0 857.9 jit_solution(9671647526459511256)
XLA Ops:
  7.2 0.0 copy-start
  7.2 0.0 copy-start.7
  7.2 0.0 copy-start.8
  7.2 0.0 copy-start.14
  7.2 0.0 all-gather.5.cloned.1.call-start
  7.3 1.1 copy-done
  8.4 19.6 %fusion.54 = (f32[450]{0:T(512)S(1)}, f32[450]{0:T(512)S(1)}, f32[4096,450]{0,1:T(8,128)}) fusion(f32[450]{0:T(512)} %param.16, bf16[450,1024]{1,0:T(8,128)(2,1)S(1)} %copy-done, s32[1024]{0:T(1024)} %param.14, s32[1024]{0:T(1024)} %param.13, s32[4096]{0:T(1024)} %param.12), kind=kOutput, calls=%fused_computation.82 | convolution fusion | flops 3845479424 | bytes 8324376 | tf_op jit(solution)/shard_map/dot_general | solution.py:42
  28.0 11.8 %all-reduce.3 = (f32[450]{0:T(512)S(1)}, f32[450]{0:T(512)S(1)}) all-reduce(f32[450]{0:T(512)S(1)} %get-tuple-element.12, f32[450]{0:T(512)S(1)} %get-tuple-element.11), channel_id=1, replica_groups=mesh['dp'=8,'mp'=4] {'dp'}, use_global_device_ids=true, to_apply=%region_3.4 | all-reduce | flops 900 | bytes 7200 | tf_op jit(solution)/shard_map/psum | solution.py:48
  39.8 0.0 copy-done.8
  39.8 0.0 copy-done.7
  39.9 0.0 copy-done.14
  39.9 0.0 copy-start.2
  39.9 10.2 %fusion.68 = bf16[1,450,4096]{2,1,0:T(8,128)(2,1)} fusion(f32[450]{0:T(512)S(1)} %copy-done.14, f32[450]{0:T(512)S(1)} %copy-done.8, f32[450]{0:T(512)S(1)} %get-tuple-element.33, f32[450]{0:T(512)S(1)} %get-tuple-element.36, f32[4096,450]{0,1:T(8,128)} %get-tuple-element.38, f32[450]{0:T(512)S(1)} %copy-done.7), kind=kLoop, calls=%fused_computation.86 | loop fusion | flops 23961600 | bytes 11068200
  50.1 0.0 all-gather.5.cloned.1.call-update
  50.1 0.0 all-gather.7.cloned.1.call-start
  50.2 0.0 copy-done.2
  50.2 3.7 all_to_all.14
  53.9 3.0 copy.24
  56.9 93.6 %all_to_all.19 = bf16[450,4,450]{0,2,1:T(8,128)(2,1)S(1)} all-to-all(bf16[450,4,450]{0,2,1:T(8,128)(2,1)S(1)} %copy.24), channel_id=1, replica_groups=mesh['dp'=8,'mp'=4] {'mp'}, dimensions={1} | all-to-all | bytes 3240000 | tf_op jit(solution)/shard_map/all_to_all | solution.py:55
  150.6 0.9 copy.25
  151.5 3.6 all_to_all.17
  155.1 0.0 copy-start.4
  155.1 0.0 copy-start.5
  155.1 187.9 %all-gather.5.cloned.1.call-done = bf16[4,450,4096]{2,1,0:T(8,128)(2,1)} async-done(((bf16[1,450,4096]{2,1,0:T(8,128)(2,1)}), bf16[4,450,4096]{2,1,0:T(8,128)(2,1)}) %all-gather.5.cloned.1.call-update) | async-done | bytes 14745616 | tf_op jit(solution)/shard_map/all_gather | solution.py:59
  343.0 14.2 %reshape.55 = bf16[1800,4096]{1,0:T(8,128)(2,1)} reshape(bf16[4,450,4096]{2,1,0:T(8,128)(2,1)} %all-gather.5.cloned.1.call-done) | data formatting | bytes 29491200
  357.3 0.0 copy-done.4
  357.3 0.0 copy-done.5
  357.3 18.2 %fusion.55 = (f32[450]{0:T(512)S(1)}, f32[450]{0:T(512)S(1)}, f32[4096,450]{0,1:T(8,128)}) fusion(f32[450]{0:T(512)S(1)} %copy-done.5, bf16[1800,4096]{1,0:T(8,128)(2,1)} %reshape.55, bf16[1800,450]{0,1:T(8,128)(2,1)S(1)} %copy-done.4), kind=kOutput, calls=%fused_computation.83 | convolution fusion | flops 6655794176 | bytes 23743800 | tf_op jit(solution)/shard_map/dot_general | solution.py:57
  375.5 11.6 %all-reduce.2 = (f32[450]{0:T(512)S(1)}, f32[450]{0:T(512)S(1)}) all-reduce(f32[450]{0:T(512)S(1)} %get-tuple-element.10, f32[450]{0:T(512)S(1)} %get-tuple-element.9), channel_id=1, replica_groups=mesh['dp'=8,'mp'=4] {'dp'}, use_global_device_ids=true, to_apply=%region_7.8 | all-reduce | flops 900 | bytes 7200 | tf_op jit(solution)/shard_map/psum | solution.py:66
  387.1 0.0 copy-done.6
  387.1 0.0 copy-done.9
  387.1 12.2 %convert_reduce_fusion = (f32[450]{0:T(512)S(1)}, f32[450]{0:T(512)S(1)}, bf16[450,4096]{1,0:T(8,128)(2,1)}) fusion(bf16[450,4096]{1,0:T(8,128)(2,1)} %param.23, f32[450]{0:T(512)S(1)} %get-tuple-element.35, f32[450]{0:T(512)S(1)} %get-tuple-element.37, f32[4096,450]{0,1:T(8,128)} %get-tuple-element.39, f32[450]{0:T(512)S(1)} %copy-done.5, ...), kind=kLoop, calls=%fused_computation.13 | loop fusion | flops 31333500 | bytes 14758200 | tf_op jit(solution)/shard_map/reduce_sum | solution.py:74
  399.3 13.5 %all-reduce.1 = (f32[450]{0:T(512)S(1)}, f32[450]{0:T(512)S(1)}) all-reduce(f32[450]{0:T(512)S(1)} %get-tuple-element.14, f32[450]{0:T(512)S(1)} %get-tuple-element.13), channel_id=1, replica_groups=mesh['dp'=8,'mp'=4] {'dp'}, use_global_device_ids=true, to_apply=%region_11.12 | all-reduce | flops 900 | bytes 7200 | tf_op jit(solution)/shard_map/psum | solution.py:74
  412.8 14.2 %fusion.56 = (bf16[450]{0:T(512)(128)(2,1)S(1)}, bf16[450,4096]{1,0:T(8,128)(2,1)}) fusion(f32[450]{0:T(512)S(1)} %get-tuple-element.17, f32[450]{0:T(512)S(1)} %get-tuple-element.35, f32[450]{0:T(512)S(1)} %get-tuple-element.37, f32[4096,450]{0,1:T(8,128)} %get-tuple-element.39, f32[450]{0:T(512)S(1)} %copy-done.5, f32[450]{0:T(512)S(1)} %broadcast_multiply_fusion.1, ...), kind=kLoop, calls=%fused_computation.84 | loop fusion | flops 49765952 | bytes 14757300 | tf_op jit(solution)/shard_map/reduce_sum | solution.py:77
  427.0 0.0 copy-done.10
  427.0 0.0 copy-done.12
  427.0 0.0 all-gather.7.cloned.1.call-update
  427.0 0.0 all-reduce.8.cloned.1.call-start
  427.1 254.3 %all-gather.7.cloned.1.call-done = bf16[4,450,4096]{2,1,0:T(8,128)(2,1)} async-done(((bf16[1,450,4096]{2,1,0:T(8,128)(2,1)}), bf16[4,450,4096]{2,1,0:T(8,128)(2,1)}) %all-gather.7.cloned.1.call-update) | async-done | bytes 14745616 | tf_op jit(solution)/shard_map/all_gather | solution.py:78
  681.4 14.2 %reshape.57 = bf16[1800,4096]{1,0:T(8,128)(2,1)} reshape(bf16[4,450,4096]{2,1,0:T(8,128)(2,1)} %all-gather.7.cloned.1.call-done) | data formatting | bytes 29491200
  695.6 20.6 %convolution_convert_fusion = bf16[450,1800]{1,0:T(8,128)(2,1)} fusion(bf16[1800,4096]{1,0:T(8,128)(2,1)} %reshape.57, f32[450]{0:T(512)S(1)} %copy-done.14, f32[450]{0:T(512)S(1)} %copy-done.8, f32[450]{0:T(512)S(1)} %get-tuple-element.33, f32[450]{0:T(512)S(1)} %get-tuple-element.36, f32[4096,450]{0,1:T(8,128)} %get-tuple-element.38, f32[450]{0:T(512)S(1)} %copy-done.7), kind=kOutput, calls=%fused_computation.64 | convolution fusion | flops 6660291584 | bytes 23747400 | tf_op jit(solution)/shard_map/dot_general | solution.py:80
  716.2 0.0 copy-done.3
  716.2 19.2 %fusion.22 = (f32[450]{0:T(512)S(1)}, f32[4096,450]{0,1:T(8,128)}) fusion(f32[450]{0:T(512)S(1)} %get-tuple-element.33, f32[450]{0:T(512)S(1)} %get-tuple-element.36, f32[4096,450]{0,1:T(8,128)} %get-tuple-element.38, f32[450]{0:T(512)S(1)} %copy-done.7, bf16[1800,4096]{1,0:T(8,128)(2,1)} %reshape.57, bf16[450,1800]{1,0:T(8,128)(2,1)S(1)} %copy-done.3), kind=kOutput, calls=%fused_computation.29 | convolution fusion | flops 6657637888 | bytes 31118400 | tf_op jit(solution)/shard_map/dot_general | solution.py:79
  735.4 3.5 reduce_sum.102
  738.9 11.7 %all-reduce = (f32[450]{0:T(512)S(1)}, f32[450]{0:T(512)S(1)}) all-reduce(f32[450]{0:T(512)S(1)} %get-tuple-element.40, f32[450]{0:T(512)S(1)} %reduce_sum.102), channel_id=1, replica_groups=mesh['dp'=8,'mp'=4] {'dp'}, use_global_device_ids=true, to_apply=%region_15.16 | all-reduce | flops 900 | bytes 7200 | tf_op jit(solution)/shard_map/psum | solution.py:88
  750.7 0.0 copy-start.15
  750.7 0.0 copy-start.16
  750.7 0.0 copy-start.17
  750.7 13.8 %fusion.58 = (bf16[450]{0:T(512)(128)(2,1)S(1)}, bf16[450,4096]{1,0:T(8,128)(2,1)S(1)}) fusion(f32[450]{0:T(512)S(1)} %get-tuple-element.15, f32[450]{0:T(512)S(1)} %get-tuple-element.33, f32[450]{0:T(512)S(1)} %get-tuple-element.36, f32[4096,450]{0,1:T(8,128)} %get-tuple-element.38, f32[450]{0:T(512)S(1)} %copy-done.7, f32[450]{0:T(512)S(1)} %broadcast_multiply_fusion, ...), kind=kLoop, calls=%fused_computation.85 | loop fusion | flops 47922752 | bytes 18443700 | tf_op jit(solution)/shard_map/reduce_sum | solution.py:91
  764.6 0.0 copy-done.11
  764.6 0.0 copy-done.13
  764.6 0.0 copy-done.15
  764.6 0.0 copy-done.16
  764.6 0.0 copy-done.17
  764.6 0.0 copy-start.1
  764.6 13.6 %fusion.41 = bf16[450,1024]{1,0:T(8,128)(2,1)} fusion(bf16[450,4096]{1,0:T(8,128)(2,1)S(1)} %get-tuple-element.30, s32[1024]{0:T(1024)S(1)} %copy-done.16, s32[1024]{0:T(1024)S(1)} %copy-done.17, s32[4096]{0:T(1024)S(1)} %copy-done.15), kind=kOutput, calls=%fused_computation.65 | convolution fusion | flops 3825666048 | bytes 4632576 | tf_op jit(solution)/shard_map/dot_general | solution.py:92
  778.3 0.0 all-reduce.8.cloned.1.call-update
  778.3 14.0 %all-reduce.4 = (bf16[450]{0:T(512)(128)(2,1)S(1)}, bf16[450]{0:T(512)(128)(2,1)S(1)}) all-reduce(bf16[450]{0:T(512)(128)(2,1)S(1)} %get-tuple-element.29, bf16[450]{0:T(512)(128)(2,1)S(1)} %get-tuple-element.27), channel_id=1, replica_groups=mesh['dp'=8,'mp'=4] {'dp'}, use_global_device_ids=true, to_apply=%region_18.19 | all-reduce | flops 900 | bytes 3600 | tf_op jit(solution)/shard_map/psum | solution.py:95
  792.3 0.6 convert_element_type.52
  792.9 0.6 convert_element_type.55
  793.5 51.6 %all-reduce.8.cloned.1.call-done = (bf16[450,1024]{1,0:T(8,128)(2,1)}, bf16[450,1800]{1,0:T(8,128)(2,1)}) async-done(((bf16[450,1024]{1,0:T(8,128)(2,1)}, bf16[450,1800]{1,0:T(8,128)(2,1)}), (bf16[450,1024]{1,0:T(8,128)(2,1)}, bf16[450,1800]{1,0:T(8,128)(2,1)})) %all-reduce.8.cloned.1.call-update) | async-done | bytes 2541616 | tf_op jit(solution)/shard_map/psum | solution.py:94
  845.1 2.6 convert_element_type.51
  847.7 3.5 convert_element_type.54
  851.2 0.0 copy-done.1
  (11 shorter events, 0.0 us)
Async XLA Ops:
  7.2 1.2 copy-start
  7.2 32.7 %copy-start.7 = (f32[450]{0:T(512)S(1)}, f32[450]{0:T(512)}, u32[]{:S(2)}) copy-start(f32[450]{0:T(512)} %param.16) | copy-start | bytes 5404
  7.2 32.6 %copy-start.8 = (f32[450]{0:T(512)S(1)}, f32[450]{0:T(512)}, u32[]{:S(2)}) copy-start(f32[450]{0:T(512)} %param.17) | copy-start | bytes 5404
  7.2 32.6 %copy-start.14 = (f32[450]{0:T(512)S(1)}, f32[450]{0:T(512)}, u32[]{:S(2)}) copy-start(f32[450]{0:T(512)} %param.18) | copy-start | bytes 5404
  7.2 335.8 %all-gather.5.cloned.1.call-start = ((), (), s32[]{:S(2)}) async-start(), calls=%async_computation.1 | async-start | bytes 18677760 | tf_op jit(solution)/shard_map/all_gather | solution.py:59
  39.9 10.3 %copy-start.2 = (bf16[450,1800]{1,0:T(8,128)(2,1)S(1)}, bf16[450,1800]{1,0:T(8,128)(2,1)}, u32[]{:S(2)}) copy-start(bf16[450,1800]{1,0:T(8,128)(2,1)} %param.19) | copy-start | bytes 4860004
  50.1 631.3 %all-gather.7.cloned.1.call-start = ((), (), s32[]{:S(2)}) async-start(), calls=%async_computation.2 | async-start | bytes 18677760 | tf_op jit(solution)/shard_map/all_gather | solution.py:78
  155.1 202.1 %copy-start.4 = (bf16[1800,450]{0,1:T(8,128)(2,1)S(1)}, bf16[1800,450]{0,1:T(8,128)(2,1)}, u32[]{:S(2)}) copy-start(bf16[1800,450]{0,1:T(8,128)(2,1)} %all_to_all.17) | copy-start | bytes 4860004
  155.1 202.1 %copy-start.5 = (f32[450]{0:T(512)S(1)}, f32[450]{0:T(512)}, u32[]{:S(2)}) copy-start(f32[450]{0:T(512)} %param.20) | copy-start | bytes 5404
  357.3 29.8 %copy-start.6 = (f32[450]{0:T(512)S(1)}, f32[450]{0:T(512)}, u32[]{:S(2)}) copy-start(f32[450]{0:T(512)} %param.21) | copy-start | bytes 5404
  357.3 29.8 %copy-start.9 = (f32[450]{0:T(512)S(1)}, f32[450]{0:T(512)}, u32[]{:S(2)}) copy-start(f32[450]{0:T(512)} %param.22) | copy-start | bytes 5404
  412.8 14.2 %copy-start.10 = (f32[450]{0:T(512)}, f32[450]{0:T(512)S(1)}, u32[]{:S(2)}) copy-start(f32[450]{0:T(512)S(1)} %get-tuple-element.17) | copy-start | bytes 5404
  412.8 14.2 %copy-start.12 = (f32[450]{0:T(512)}, f32[450]{0:T(512)S(1)}, u32[]{:S(2)}) copy-start(f32[450]{0:T(512)S(1)} %get-tuple-element.18) | copy-start | bytes 5404
  427.0 418.1 %all-reduce.8.cloned.1.call-start = ((), (), s32[]{:S(2)}) async-start(), calls=%async_computation.3 | async-start | bytes 5369856 | tf_op jit(solution)/shard_map/psum | solution.py:94
  695.6 20.6 %copy-start.3 = (bf16[450,1800]{1,0:T(8,128)(2,1)S(1)}, bf16[450,1800]{1,0:T(8,128)(2,1)}, u32[]{:S(2)}) copy-start(bf16[450,1800]{1,0:T(8,128)(2,1)} %param.19) | copy-start | bytes 4860004
  750.7 13.9 %copy-start.11 = (f32[450]{0:T(512)}, f32[450]{0:T(512)S(1)}, u32[]{:S(2)}) copy-start(f32[450]{0:T(512)S(1)} %get-tuple-element.15) | copy-start | bytes 5404
  750.7 13.9 %copy-start.13 = (f32[450]{0:T(512)}, f32[450]{0:T(512)S(1)}, u32[]{:S(2)}) copy-start(f32[450]{0:T(512)S(1)} %get-tuple-element.16) | copy-start | bytes 5404
  750.7 13.9 %copy-start.15 = (s32[4096]{0:T(1024)S(1)}, s32[4096]{0:T(1024)}, u32[]{:S(2)}) copy-start(s32[4096]{0:T(1024)} %param.12) | copy-start | bytes 49156
  750.7 13.9 %copy-start.16 = (s32[1024]{0:T(1024)S(1)}, s32[1024]{0:T(1024)}, u32[]{:S(2)}) copy-start(s32[1024]{0:T(1024)} %param.14) | copy-start | bytes 12292
  750.7 13.9 %copy-start.17 = (s32[1024]{0:T(1024)S(1)}, s32[1024]{0:T(1024)}, u32[]{:S(2)}) copy-start(s32[1024]{0:T(1024)} %param.13) | copy-start | bytes 12292
  764.6 86.6 %copy-start.1 = (bf16[450,1024]{1,0:T(8,128)(2,1)S(1)}, bf16[450,1024]{1,0:T(8,128)(2,1)}, u32[]{:S(2)}) copy-start(bf16[450,1024]{1,0:T(8,128)(2,1)} %param.15) | copy-start | bytes 2764804
Sparse Core Ops, SparseCore 0:
  50.2 292.7 all-gather.4
  427.1 254.2 all-gather.6
  778.4 66.6 all-reduce.7
where the time goes:
time: 868 us; the launch traced here: 858 us
  waiting for transfers between devices  494 us (57%)
  blocking collectives  156 us (18%)
  matrix products  91.3 us (11%)
  other arithmetic  61.2 us (7%)
  local copies, waits for them, and re-layouts  41 us (5%)
  between operations  14.1 us (2%)
    all_gather x1, waiting for transfers between devices, per_device(): piece = lax.all_gather(d_pre_second, 'mp', axis=0, tiled=True)  254 us
    all_gather x1, waiting for transfers between devices, per_device(): lax.all_gather(hidden, 'mp', axis=0, tiled=True)  188 us
    all_to_all x1, blocking collectives, per_device(): lax.all_to_all(weight_second, 'mp', split_axis=1, concat_axis=0, tiled=True)  93.6 us
    psum x1, waiting for transfers between devices, per_device(): lax.psum(local_weight_first.astype(jnp.bfloat16), 'dp').astype(jnp.float32)  51.6 us
    unnamed x38, local copies, waits for them, and re-layouts  29.7 us
    dot_general x1, matrix products, per_device(): lax.dot_general(hidden, piece, (((1,), (1,)), ((), ())), preferred_elemen...  20.6 us
    dot_general x1, matrix products, per_device(): lax.dot_general(weight_first, encoding, (((1,), (1,)), ((), ())), preferr...  19.6 us
    dot_general x1, matrix products, per_device(): d_hidden = jnp.dot(weight_second, piece, preferred_element_type=jnp.float32)  19.2 us
  transfers between devices with their start and end apart: 3, of which 3 were waited for; matrix products, arithmetic and copies ran while one was open for 1% of the time, Pallas kernels for 0%

commit v1 on v0

v1 whole, which is shorter than its diff:
```python
import functools

import jax
import jax.numpy as jnp
from jax import lax
from jax.experimental import pallas as pl
from jax.experimental.pallas import tpu as pltpu
from jax.sharding import PartitionSpec as P

MESH = pl.DeviceIdType.MESH
F32, BF16, I32 = jnp.float32, jnp.bfloat16, jnp.int32
epsilon = 1e-05


def dot(a, b):
    return lax.dot_general(a, b, (((1,), (0,)), ((), ())), preferred_element_type=F32)


def dot_nt(a, b):
    return lax.dot_general(a, b, (((1,), (1,)), ((), ())), preferred_element_type=F32)


def mish_parts(v):
    u = jnp.exp(jnp.minimum(v, 20.0))
    n = u * (u + 2.0)
    d = n + 2.0
    r = pl.reciprocal(d, approx=True)
    r = r * (2.0 - d * r)
    t = n * r
    return v * t, t + v * ((4.0 * (n - u) * r) * r)


def mish(v):
    u = jnp.exp(jnp.minimum(v, 20.0))
    n = u * (u + 2.0)
    d = n + 2.0
    r = pl.reciprocal(d, approx=True)
    r = r * (2.0 - d * r)
    return v * (n * r)


def lane_part(x):
    out = x[:, :128]
    for at in range(128, x.shape[1], 128):
        out = out + x[:, at : at + 128]
    return out


def kernel(
    D, M, U, LP, K, R,
    ids_ref, mult_ref, add_ref, par_ref, w1_ref, w2_ref, cot_ref,
    out_ref, gw1_ref, gw2_ref, vec_ref,
    A, B, C, W2, E1, F, H, act2, slo2, G1, col, RW, acc, T, hcol,
    pv, ar1, ar2, ar2z, ar3, ar3z, ar4, ar4s, ar4z,
    w1s, w1r, w2s, w2r, pvs, pvr, cts, ctr, loc,
    a1s, a1r, a2s, a2r, a2zs, a2zr, a3s, a3r, a3zs, a3zr, a4s, a4r, a4zs, a4zr,
    g1s, g1r, g2s, g2r, *extra,
):
    Q = R // M
    G = D // 8
    TL = min(512, Q)
    NT = Q // TL
    PER = K // LP
    NA = M // PER
    K8 = K // 8
    J8 = M * LP // 8
    S8 = LP // 8
    N = float(R * D)
    d = lax.axis_index("dp")
    m = lax.axis_index("mp")
    i = lax.rem(d, 8)
    c = lax.rem(i, 2)
    x = lax.rem(i // 2, 2)
    y = i // 4
    hi = (1 - c) * x + c * y
    lo = (1 - c) * y + c * x
    p = 4 * c + 2 * hi + lo
    core_dev = (d + 1 - 2 * c, m)
    flip_x = d + 2 - 4 * x
    flip_y = d + 4 - 8 * y
    hi_dev = ((1 - c) * flip_x + c * flip_y, m)
    lo_dev = ((1 - c) * flip_y + c * flip_x, m)
    up = [lax.rem(m + k, M) for k in range(M)]
    down = [lax.rem(m - k + M, M) for k in range(M)]
    others = [lax.rem(d + k, D) for k in range(D)]
    sent = []

    def remote(src, dst, ss, rs, dev):
        cp = pltpu.make_async_remote_copy(
            src_ref=src, dst_ref=dst, send_sem=ss, recv_sem=rs, device_id=dev, device_id_type=MESH
        )
        return cp

    def send(src, dst, ss, rs, dev):
        cp = remote(src, dst, ss, rs, dev)
        cp.start()
        sent.append(cp)
        return cp

    def gone(cp):
        cp.wait_send()
        sent[:] = [other for other in sent if other is not cp]

    def lanes(ref, at, size):
        return ref.at[:, pl.ds(pl.multiple_of(at, 128), size)]

    def rows(ref, at, size):
        return ref.at[pl.ds(pl.multiple_of(at, 16), size)]

    bar = pltpu.get_barrier_semaphore()
    for k in range(1, D):
        pl.semaphore_signal(bar, inc=1, device_id=(others[k], m), device_id_type=MESH)
    for k in range(1, M):
        pl.semaphore_signal(bar, inc=1, device_id=(d, up[k]), device_id_type=MESH)

    w1_loc = pltpu.make_async_copy(w1_ref, C.at[m], loc.at[0])
    w1_loc.start()
    w2_loc = pltpu.make_async_copy(w2_ref, W2.at[m], loc.at[1])
    w2_loc.start()
    cot_loc = pltpu.make_async_copy(lanes(cot_ref, m * Q, Q), lanes(F.at[m], 0, Q), loc.at[2])
    cot_loc.start()
    pv[m] = par_ref[...]
    pl.semaphore_wait(bar, D - 1 + M - 1)

    ag1, ag2, agp, ct = {}, {}, {}, {}
    for k in range(1, M):
        agp[k] = send(par_ref, pv.at[m], pvs.at[k], pvr.at[k], (d, up[k]))
    for k in range(1, M):
        ag1[0, k] = send(
            lanes(w1_ref, p * K8, K8), lanes(C.at[m], p * K8, K8), w1s.at[0, k], w1r.at[0, k], (d, up[k])
        )
    for k in range(1, M):
        ag2[0, k] = send(
            lanes(w2_ref, p * J8, J8), lanes(W2.at[m], p * J8, J8), w2s.at[0, k], w2r.at[0, k], (d, up[k])
        )
    for k in range(1, M):
        ct[k] = send(lanes(cot_ref, up[k] * Q, Q), lanes(F.at[m], 0, Q), cts.at[k], ctr.at[k], (d, up[k]))

    def gather_stage(step, ag, buf, size, ss, rs):
        dev, at, width = {
            1: (lo_dev, p * size, size),
            2: (hi_dev, (4 * c + 2 * hi) * size, 2 * size),
            3: (core_dev, 4 * c * size, 4 * size),
        }[step]
        for k in range(1, M):
            ag[step - 1, k].wait_recv()
            part = lanes(buf.at[down[k]], at, width)
            ag[step, k] = send(part, part, ss.at[step, k], rs.at[step, k], dev)

    def stage1(step):
        gather_stage(step, ag1, C, K8, w1s, w1r)

    def stage2(step):
        gather_stage(step, ag2, W2, J8, w2s, w2r)

    hrow = jnp.concatenate(
        [mult_ref[...].astype(F32), add_ref[...].astype(F32), jnp.zeros((126, K), F32)], axis=0
    )
    hcol[...] = hrow.T

    HT = 128

    def encode(q, slot):
        def step(t, _):
            at = pl.multiple_of(t * HT, HT)
            both = hcol[pl.ds(at, HT), :].astype(I32)
            v = both[:, 0:1] * ids_ref[:, pl.ds(pl.multiple_of(q * Q, 128), Q)] + both[:, 1:2]
            for _ in range(2):
                top = lax.shift_right_logical(v, 16)
                v = (v & 65535) + ((top << 4) - top)
            v = jnp.where(v >= 65521, v - 65521, v)
            A[slot, pl.ds(at, HT), :] = (v.astype(F32) * (2.0 / 65520.0) - 1.0).astype(BF16)
            return 0

        lax.fori_loop(0, K // HT, step, 0)

    def make_cols():
        def step(b, _):
            col[b] = jnp.concatenate([RW[b], jnp.zeros((128 - RW.shape[1], LP), F32)], axis=0).T
            return 0

        lax.fori_loop(0, M, step, 0)

    def row_of(slot):
        return jnp.sum(acc[slot].T, axis=0, keepdims=True)

    acc[...] = jnp.zeros_like(acc)
    for b in range(M):
        B[pl.ds(b * LP + U // 16 * 16, LP - U // 16 * 16), :] = jnp.zeros((LP - U // 16 * 16, R), BF16)

    encode(m, m)
    encode(down[1], down[1])
    stage1(1)

    def enc_step(k, _):
        q = lax.rem(m + M - k, M)
        encode(q, q)
        return 0

    lax.fori_loop(2, M, enc_step, 0)
    stage1(2)
    for k in range(1, M):
        agp[k].wait_recv()
    for b in range(M):
        RW[b, 0:8] = pv[b]
        RW[b, 8:32] = jnp.zeros((24, LP), F32)
    make_cols()
    w1_loc.wait()

    def mm1_own(b):
        def step(t, _):
            at = pl.multiple_of(t * TL, TL)
            v = dot(C[b], A[m, :, pl.ds(at, TL)]) + col[b, :U, 0:1]
            act, slope = mish_parts(v)
            H[b, :, pl.ds(at, TL)] = slope.astype(BF16)
            B[pl.ds(pl.multiple_of(b * LP, LP), U), pl.ds(pl.multiple_of(m * Q + t * TL, TL), TL)] = act.astype(BF16)
            acc[0, :U] += lane_part(act)
            acc[1, :U] += lane_part(act * act)
            return 0

        lax.fori_loop(0, NT, step, 0)

    def mm1_rest(b):
        def step(t, _):
            q = lax.rem(m + 1 + t // NT, M)
            at = pl.multiple_of(lax.rem(t, NT) * TL, TL)
            act = mish(dot(C[b], A[q, :, pl.ds(at, TL)]) + col[b, :U, 0:1])
            B[pl.ds(pl.multiple_of(b * LP, LP), U), pl.ds(pl.multiple_of(q * Q + at, TL), TL)] = act.astype(BF16)
            acc[0, :U] += lane_part(act)
            acc[1, :U] += lane_part(act * act)
            return 0

        lax.fori_loop(0, (M - 1) * NT, step, 0)

    def mm1(b):
        mm1_own(b)
        mm1_rest(b)
        ar1[d, pl.ds(b, 1), :] = row_of(0)
        ar1[d, pl.ds(b + M, 1), :] = row_of(1)
        acc[0:2] = jnp.zeros((2, LP, 128), F32)

    mm1(m)
    stage2(1)
    stage1(3)
    for k in range(1, M):
        ag1[3, k].wait_recv()
        mm1(down[k])
        if k == 1:
            stage2(2)
        if k == 2:
            stage2(3)

    def all_dp(buf, ss, rs):
        cps = []
        for k in range(1, D):
            cps.append(send(buf.at[d], buf.at[d], ss.at[k], rs.at[k], (others[k], m)))
        return cps

    def total(buf, cps):
        for cp in cps:
            cp.wait_recv()
        out = buf[0]
        for k in range(1, D):
            out = out + buf[k]
        return out

    cps1 = all_dp(ar1, a1s, a1r)
    for step in range(1, 4):
        for k in range(1, M):
            gone(ag1[step, k])
    cot_all = []
    for q in range(M):
        cp = pltpu.make_async_copy(lanes(cot_ref, q * Q, Q), lanes(C.at[q], 0, Q), loc.at[3 + q])
        cot_all.append(cp)
        cp.start()
    w2_loc.wait()
    for k in range(1, M):
        ag2[3, k].wait_recv()

    T[...] = jnp.zeros_like(T)

    def make_e1(b):
        def step(h, _):
            T[:U, :] = W2[h, :, pl.ds(pl.multiple_of(b * LP, LP), LP)].astype(F32) * col[h, :U, 1:2]
            E1[:, pl.ds(pl.multiple_of(h * LP, LP), LP)] = T[...].T.astype(BF16)
            return 0

        lax.fori_loop(0, M, step, 0)

    const = jnp.zeros((8, M * LP), F32)
    for b in range(M):
        shift = jnp.broadcast_to(pv[b, 2:3, :U], (8, U))
        upper = shift.astype(BF16)
        lower = (shift - upper.astype(F32)).astype(BF16)
        const = const + dot(upper, W2[b]) + dot(lower, W2[b])
    for b in range(M):
        RW[b, 8:9] = const[0:1, b * LP : (b + 1) * LP] + pv[b, 3:4]
    make_e1(m)

    tot = total(ar1, cps1)
    mean = tot[:M] / N
    inv = lax.rsqrt(tot[M:] / N - mean * mean + epsilon)
    for b in range(M):
        RW[b, 9:10] = inv[b : b + 1]
        RW[b, 10:11] = -mean[b : b + 1] * inv[b : b + 1]
    make_cols()
    for cp in cot_all:
        cp.wait()

    def mm2(t, _):
        at = pl.multiple_of(t * TL, TL)
        for b in range(M):
            part = B[b * LP : b * LP + U, pl.ds(at, TL)].astype(F32)
            B[b * LP : b * LP + U, pl.ds(at, TL)] = (part * col[b, :U, 9:10] + col[b, :U, 10:11]).astype(BF16)
        v = dot(E1[:U], B[:, pl.ds(at, TL)]) + col[m, :U, 8:9]
        act, slope = mish_parts(v)
        act2[:, pl.ds(at, TL)] = act.astype(BF16)
        slo2[:, pl.ds(at, TL)] = slope.astype(BF16)
        g = C[t // NT, :, pl.ds(pl.multiple_of(lax.rem(t, NT) * TL, TL), TL)].astype(F32)
        acc[0, :U] += lane_part(act)
        acc[1, :U] += lane_part(act * act)
        acc[2, :U] += lane_part(g)
        acc[3, :U] += lane_part(g * act)
        return 0

    lax.fori_loop(0, M * NT, mm2, 0)
    for s in range(4):
        ar2[d, s : s + 1, :] = row_of(s)
    ar2[d, 4:8, :] = jnp.zeros((4, LP), F32)
    acc[...] = jnp.zeros_like(acc)
    cps2 = all_dp(ar2, a2s, a2r)

    def a_at(base, b):
        return base + b // PER, pl.multiple_of(lax.rem(b, PER) * LP, LP)

    def mm2_own(b):
        make_e1(b)
        act_at, row = a_at(0, b)

        def step(t, _):
            at = pl.multiple_of(t * TL, TL)
            v = dot(E1[:U], B[:, pl.ds(pl.multiple_of(m * Q + t * TL, TL), TL)]) + col[b, :U, 8:9]
            act, slope = mish_parts(v)
            A[act_at, pl.ds(row, U), pl.ds(at, TL)] = act.astype(BF16)
            A[act_at + NA, pl.ds(row, U), pl.ds(at, TL)] = slope.astype(BF16)
            return 0

        lax.fori_loop(0, NT, step, 0)

    def own_loop(k, _):
        mm2_own(lax.rem(m + k, M))
        return 0

    mm2_own(up[1])
    tot = total(ar2, cps2)
    mean = tot[0:1] / N
    inv = lax.rsqrt(tot[1:2] / N - mean * mean + epsilon)
    sum_g = tot[2:3]
    sum_gn = inv * (tot[3:4] - mean * sum_g)
    k1 = pv[m, 4:5] * inv
    k2 = -k1 * inv * sum_gn / N
    k3 = -k1 * sum_g / N - mean * k2
    ar2z[m, 0:1] = k1
    ar2z[m, 1:2] = k2
    ar2z[m, 2:3] = k3
    ar2z[m, 3:4] = k1
    ar2z[m, 4:5] = pv[m, 5:6] - mean * k1
    ar2z[m, 5:6] = sum_g
    ar2z[m, 6:7] = sum_gn
    ar2z[m, 7:8] = jnp.zeros((1, LP), F32)
    cps2z = [send(ar2z.at[m], ar2z.at[m], a2zs.at[k], a2zr.at[k], (d, up[k])) for k in range(1, M)]
    lax.fori_loop(2, M, own_loop, 0)
    for cp in cps2z:
        cp.wait_recv()
    for b in range(M):
        RW[b, 16:24] = ar2z[b]
    make_cols()

    def back2(t, _):
        at = pl.multiple_of(t * TL, TL)
        a = act2[:, pl.ds(at, TL)].astype(F32)
        g = C[t // NT, :, pl.ds(pl.multiple_of(lax.rem(t, NT) * TL, TL), TL)].astype(F32)
        act2[:, pl.ds(at, TL)] = (a * col[m, :U, 19:20] + col[m, :U, 20:21]).astype(BF16)
        grad = (g * col[m, :U, 16:17] + a * col[m, :U, 17:18] + col[m, :U, 18:19]) * slo2[:, pl.ds(at, TL)].astype(F32)
        grad = grad.astype(BF16)
        slo2[:, pl.ds(at, TL)] = grad
        acc[0, :U] += lane_part(grad.astype(F32))
        return 0

    lax.fori_loop(0, M * NT, back2, 0)
    out_copy = pltpu.make_async_copy(act2, out_ref, loc.at[0])
    out_copy.start()
    gb2 = row_of(0)
    ar3[d, 2 * M : 2 * M + 1, :] = gb2
    ar3[d, 2 * M + 1 : 2 * M + 8, :] = jnp.zeros((7, LP), F32)
    acc[0:1] = jnp.zeros((1, LP, 128), F32)

    PADAT = U // 16 * 16

    def put_grad(b, value, at, size):
        slot, row = a_at(NA, b)
        A[slot, pl.ds(row, U), pl.ds(at, size)] = value

    for b in range(M):
        slot, row = NA + b // PER, (b % PER) * LP
        A[slot, row + PADAT : row + LP, :] = jnp.where(
            lax.broadcasted_iota(I32, (LP - PADAT, Q), 0) < U - PADAT,
            A[slot, row + PADAT : row + LP, :].astype(F32),
            0.0,
        ).astype(BF16)
    cot_loc.wait()

    def back2_own(b):
        act_at, row = a_at(0, b)

        def step(t, _):
            at = pl.multiple_of(t * TL, TL)
            a = A[act_at, pl.ds(row, U), pl.ds(at, TL)].astype(F32)
            s = A[act_at + NA, pl.ds(row, U), pl.ds(at, TL)].astype(F32)
            g = F[b, :, pl.ds(at, TL)].astype(F32)
            grad = (g * col[b, :U, 16:17] + a * col[b, :U, 17:18] + col[b, :U, 18:19]) * s
            A[act_at + NA, pl.ds(row, U), pl.ds(at, TL)] = grad.astype(BF16)
            return 0

        lax.fori_loop(0, NT, step, 0)

    def copy_own(t, _):
        at = pl.multiple_of(t * TL, TL)
        put_grad(m, slo2[:, pl.ds(pl.multiple_of(m * Q + t * TL, TL), TL)], at, TL)
        return 0

    lax.fori_loop(0, NT, copy_own, 0)
    for k in range(1, M):
        ct[k].wait_recv()
        back2_own(down[k])

    def d_hidden(b):
        def step(t, _):
            at = pl.multiple_of(t * TL, TL)
            dh = dot(W2[b, :, 0:K], A[NA, :, pl.ds(at, TL)])
            for n in range(1, NA):
                dh = dh + dot(W2[b, :, n * K : (n + 1) * K], A[NA + n, :, pl.ds(at, TL)])
            norm = B[pl.ds(pl.multiple_of(b * LP, LP), U), pl.ds(pl.multiple_of(m * Q + t * TL, TL), TL)].astype(F32)
            F[b, :, pl.ds(at, TL)] = dh.astype(BF16)
            acc[0, :U] += lane_part(dh)
            acc[1, :U] += lane_part(dh * norm)
            return 0

        lax.fori_loop(0, NT, step, 0)
        ar3[d, pl.ds(b, 1), :] = row_of(0)
        ar3[d, pl.ds(b + M, 1), :] = row_of(1)
        acc[0:2] = jnp.zeros((2, LP, 128), F32)

    def d_hidden_step(b, _):
        d_hidden(b)
        return 0

    lax.fori_loop(0, M, d_hidden_step, 0)
    for step in range(1, 4):
        for k in range(1, M):
            gone(ag2[step, k])
    cps3 = all_dp(ar3, a3s, a3r)

    def grad_w2(b, _):
        g = dot_nt(B[pl.ds(pl.multiple_of(b * LP, LP), LP), :], slo2[...])
        g = g * col[b, :, 1:2] + col[b, :, 2:3] * gb2[:, :U]
        E1[:, pl.ds(pl.multiple_of(b * LP, LP), U)] = g.astype(BF16)
        return 0

    lax.fori_loop(0, M, grad_w2, 0)
    tot = total(ar3, cps3)
    ar3z[m] = tot[: 2 * M]
    gb2_all = tot[2 * M : 2 * M + 1]
    cps3z = [send(ar3z.at[m], ar3z.at[m], a3zs.at[k], a3zr.at[k], (d, up[k])) for k in range(1, M)]
    encode(m, 0)
    for cp in cps3z:
        cp.wait_recv()
    tot = ar3z[0]
    for b in range(1, M):
        tot = tot + ar3z[b]

    R2 = W2.at[0]
    h2 = LP // 2
    g2cp = {}
    g2cp[0] = send(rows(E1, (1 - c) * h2, h2), rows(R2, 0, h2), g2s.at[0], g2r.at[0], core_dev)

    for b in range(M):
        k1 = pv[b, 1:2] * RW[b, 9:10]
        k2 = -k1 * tot[M + b : M + b + 1] / N
        k3 = -k1 * tot[b : b + 1] / N
        RW[b, 16:17] = k1
        RW[b, 17:18] = k2
        RW[b, 18:19] = k3
    make_cols()
    pick = lax.broadcasted_iota(I32, (2 * M, 1), 0)
    vec_ref[0:1, :] = jnp.zeros((1, LP), F32)
    vec_ref[1:2, :] = jnp.sum(jnp.where(pick == M + m, tot, 0.0), axis=0, keepdims=True)
    vec_ref[2:3, :] = jnp.sum(jnp.where(pick == m, tot, 0.0), axis=0, keepdims=True)
    vec_ref[3:4, :] = gb2_all
    vec_ref[4:5, :] = ar2z[m, 6:7]
    vec_ref[5:6, :] = ar2z[m, 5:6]
    vec_ref[6:8, :] = jnp.zeros((2, LP), F32)

    def back1(b):
        def step(t, _):
            at = pl.multiple_of(t * TL, TL)
            norm = B[pl.ds(pl.multiple_of(b * LP, LP), U), pl.ds(pl.multiple_of(m * Q + t * TL, TL), TL)].astype(F32)
            dh = F[b, :, pl.ds(at, TL)].astype(F32)
            grad = dh * col[b, :U, 16:17] + norm * col[b, :U, 17:18] + col[b, :U, 18:19]
            grad = (grad * H[b, :, pl.ds(at, TL)].astype(F32)).astype(BF16)
            H[b, :, pl.ds(at, TL)] = grad
            acc[0, :U] += lane_part(grad.astype(F32))
            return 0

        lax.fori_loop(0, NT, step, 0)
        ar4[d, pl.ds(b, 1), :] = row_of(0)
        acc[0:1] = jnp.zeros((1, LP, 128), F32)

        def mm(t, _):
            at = pl.multiple_of(t * TL, TL)
            F[b, :, pl.ds(at, TL)] = dot_nt(H[b], A[0, pl.ds(at, TL), :]).astype(BF16)
            return 0

        lax.fori_loop(0, K // TL, mm, 0)

    ar4[d] = jnp.zeros((ar4.shape[1], LP), F32)
    K4, K2, half = 2 * K8, 4 * K8, K // 2
    g1cp = {}
    for b in range(M):
        back1(b)
        g1cp[0, b] = send(
            lanes(F.at[b], (1 - c) * K2, K2), lanes(C.at[b], 0, K2), g1s.at[0, b], g1r.at[0, b], core_dev
        )
    cps4 = all_dp(ar4, a4s, a4r)

    def add_rows(to, at, other, size):
        def step(t, _):
            s = pl.multiple_of(t * 16, 16)
            to[pl.ds(pl.multiple_of(at + s, 16), 16), :] = (
                to[pl.ds(pl.multiple_of(at + s, 16), 16), :].astype(F32) + other(s).astype(F32)
            ).astype(BF16)
            return 0

        lax.fori_loop(0, size // 16, step, 0)

    def g2_step(n):
        g2cp[n - 1].wait_recv()
        size = h2 >> (n - 1)
        at = {1: 4 * c, 2: 4 * c + 2 * hi, 3: p}[n] * S8
        start = {1: 0, 2: h2, 3: h2 + h2 // 2}[n]
        add_rows(E1, at, lambda s: W2[0, pl.ds(pl.multiple_of(start + s, 16), 16), :], size)

    def g1_step(n, b):
        g1cp[n - 1, b].wait_recv()
        size = K2 >> (n - 1)
        at = pl.multiple_of({1: 4 * c, 2: 4 * c + 2 * hi, 3: p}[n] * K8, 128)
        start = {1: 0, 2: K2, 3: K2 + K4}[n]
        F[b, :, pl.ds(at, size)] = (
            F[b, :, pl.ds(at, size)].astype(F32) + C[b, :, start : start + size].astype(F32)
        ).astype(BF16)

    g2_step(1)
    g2cp[1] = send(
        rows(E1, (4 * c + 2 * (1 - hi)) * S8, 2 * S8), rows(R2, h2, 2 * S8), g2s.at[1], g2r.at[1], hi_dev
    )
    for b in range(M):
        g1_step(1, b)
        g1cp[1, b] = send(
            lanes(F.at[b], (4 * c + 2 * (1 - hi)) * K8, K4), lanes(C.at[b], K2, K4), g1s.at[1, b], g1r.at[1, b], hi_dev
        )
    tot4 = total(ar4, cps4)
    for b in range(M):
        ar4s[b] = jnp.broadcast_to(tot4[b : b + 1], (8, LP))
    ar4z[m] = ar4s[m]
    cps4z = [send(ar4s.at[up[k]], ar4z.at[m], a4zs.at[k], a4zr.at[k], (d, up[k])) for k in range(1, M)]
    g2_step(2)
    g2cp[2] = send(
        rows(E1, (4 * c + 2 * hi + 1 - lo) * S8, S8), rows(R2, h2 + 2 * S8, S8), g2s.at[2], g2r.at[2], lo_dev
    )
    for b in range(M):
        g1_step(2, b)
        g1cp[2, b] = send(
            lanes(F.at[b], (4 * c + 2 * hi + 1 - lo) * K8, K8), lanes(C.at[b], K2 + K4, K8), g1s.at[2, b], g1r.at[2, b], lo_dev
        )
    g2_step(3)
    for b in range(M):
        g1_step(3, b)
    if G > 1:
        x1, x2, x1s, x1r, x2s, x2r = extra
        cpsx = []
        for k in range(1, G):
            to = (lax.rem(d + 8 * k, D), m)
            cpsx.append(send(rows(E1, p * S8, S8), x2.at[d // 8], x2s.at[k], x2r.at[k], to))
            for b in range(M):
                cpsx.append(send(lanes(F.at[b], p * K8, K8), x1.at[d // 8, b], x1s.at[k, b], x1r.at[k, b], to))
        x2[d // 8] = E1[pl.ds(pl.multiple_of(p * S8, 16), S8), :]
        for b in range(M):
            x1[d // 8, b] = F[b, :, pl.ds(pl.multiple_of(p * K8, 128), K8)]
        for cp in cpsx:
            cp.wait()
        v = x2[0].astype(F32)
        for k in range(1, G):
            v = v + x2[k].astype(F32)
        E1[pl.ds(pl.multiple_of(p * S8, 16), S8), :] = v.astype(BF16)
        for b in range(M):
            v = x1[0, b].astype(F32)
            for k in range(1, G):
                v = v + x1[k, b].astype(F32)
            F[b, :, pl.ds(pl.multiple_of(p * K8, 128), K8)] = v.astype(BF16)

    g1z = [
        send(
            lanes(F.at[up[k]], p * K8, K8), C.at[m, :, pl.ds(K2 + K4 + K8, K8)], g1s.at[3, k], g1r.at[3, k], (d, up[k])
        )
        for k in range(1, M)
    ]
    Z2 = W2.at[1]
    p64 = pl.multiple_of(p * S8, 16)
    g2z = [
        send(
            E1.at[pl.ds(p64, S8), pl.ds(pl.multiple_of(up[k] * LP, LP), LP)],
            Z2.at[pl.ds(0, S8), pl.ds(pl.multiple_of(m * LP, LP), LP)],
            g2s.at[3 + k], g2r.at[3 + k], (d, up[k]),
        )
        for k in range(1, M)
    ]
    C[m, :, K2 + K4 + K8 : K] = F[m, :, pl.ds(pl.multiple_of(p * K8, 128), K8)]
    W2[1, 0:S8, pl.ds(pl.multiple_of(m * LP, LP), LP)] = E1[
        pl.ds(p64, S8), pl.ds(pl.multiple_of(m * LP, LP), LP)
    ]
    for cp in g1z:
        cp.wait_recv()
    v = C[0, :, K2 + K4 + K8 : K].astype(F32)
    for b in range(1, M):
        v = v + C[b, :, K2 + K4 + K8 : K].astype(F32)
    G1[:, pl.ds(pl.multiple_of(p * K8, 128), K8)] = v.astype(BF16)
    ga = send(lanes(G1, p * K8, K8), lanes(G1, p * K8, K8), g1s.at[4, 0], g1r.at[4, 0], lo_dev)
    for cp in g2z:
        cp.wait_recv()
    at2 = pl.multiple_of((2 * hi + lo) * S8, 16)
    W2[2 + c, pl.ds(at2, S8), :] = W2[1, 0:S8, :]
    gb = send(rows(W2.at[2 + c], at2, S8), rows(W2.at[2 + c], at2, S8), g2s.at[3 + M], g2r.at[3 + M], lo_dev)
    ga.wait_recv()
    part = lanes(G1, (4 * c + 2 * hi) * K8, K4)
    ga = send(part, part, g1s.at[4, 1], g1r.at[4, 1], hi_dev)
    gb.wait_recv()
    part = rows(W2.at[2 + c], 2 * hi * S8, 2 * S8)
    gb = send(part, part, g2s.at[4 + M], g2r.at[4 + M], hi_dev)
    ga.wait_recv()
    part = lanes(G1, 4 * c * K8, K2)
    ga = send(part, part, g1s.at[4, 2], g1r.at[4, 2], core_dev)
    gb.wait_recv()
    part = rows(W2.at[2 + c], 0, 4 * S8)
    gb = send(part, part, g2s.at[5 + M], g2r.at[5 + M], core_dev)
    for cp in cps4z:
        cp.wait_recv()
    v = ar4z[0]
    for b in range(1, M):
        v = v + ar4z[b]
    vec_ref[0:1, :] = v[0:1]
    ga.wait_recv()
    gw1_copy = pltpu.make_async_copy(G1, gw1_ref, loc.at[1])
    gw1_copy.start()
    gb.wait_recv()
    top = min(4 * S8, U)
    for b in range(M):
        slo2[0:top, b * U : (b + 1) * U] = W2[2, 0:top, b * LP : b * LP + U]
        if U > top:
            slo2[top:U, b * U : (b + 1) * U] = W2[3, 0 : U - top, b * LP : b * LP + U]
    gw2_copy = pltpu.make_async_copy(lanes(slo2, 0, gw2_ref.shape[1]), gw2_ref, loc.at[2])
    gw2_copy.start()
    out_copy.wait()
    gw1_copy.wait()
    gw2_copy.wait()
    for cp in sent:
        cp.wait_send()


def per_device(ids, hash_mult, hash_add, w1, b1, s1, t1, w2, b2, s2, t2, cot):
    D, M = lax.axis_size("dp"), lax.axis_size("mp")
    U, K = w1.shape
    R = ids.shape[0]
    Q = R // M
    LP = -(-U // 128) * 128
    G = D // 8
    par = jnp.pad(jnp.stack([b1, s1, t1, b2, s2, t2]), ((0, 2), (0, LP - U)))
    zeros = jnp.zeros((U, LP - U), BF16)
    pieces = []
    for b in range(M):
        pieces += [w2[:, b * U : (b + 1) * U], zeros]
    w2p = jnp.concatenate(pieces, axis=1)
    dma = pltpu.SemaphoreType.DMA
    vmem = pl.BlockSpec(memory_space=pltpu.VMEM)
    hbm = pl.BlockSpec(memory_space=pl.ANY)
    AR = -(-2 * M // 8) * 8
    scratch = [
        pltpu.VMEM((M, K, Q), BF16),
        pltpu.VMEM((M * LP, R), BF16),
        pltpu.VMEM((M, U, max(K, Q)), BF16),
        pltpu.VMEM((M, U, M * LP), BF16),
        pltpu.VMEM((LP, M * LP), BF16),
        pltpu.VMEM((M, U, max(K, Q)), BF16),
        pltpu.VMEM((M, U, Q), BF16),
        pltpu.VMEM((U, R), BF16),
        pltpu.VMEM((U, R), BF16),
        pltpu.VMEM((U, K), BF16),
        pltpu.VMEM((M, LP, 128), F32),
        pltpu.VMEM((M, 32, LP), F32),
        pltpu.VMEM((4, LP, 128), F32),
        pltpu.VMEM((LP, LP), F32),
        pltpu.VMEM((K, 128), F32),
        pltpu.VMEM((M, 8, LP), F32),
        pltpu.VMEM((D, AR, LP), F32),
        pltpu.VMEM((D, 8, LP), F32),
        pltpu.VMEM((M, 8, LP), F32),
        pltpu.VMEM((D, AR + 8, LP), F32),
        pltpu.VMEM((M, AR, LP), F32),
        pltpu.VMEM((D, 8, LP), F32),
        pltpu.VMEM((M, 8, LP), F32),
        pltpu.VMEM((M, 8, LP), F32),
        dma((4, M)), dma((4, M)), dma((4, M)), dma((4, M)),
        dma((M,)), dma((M,)), dma((M,)), dma((M,)), dma((3 + M,)),
        dma((D,)), dma((D,)), dma((D,)), dma((D,)), dma((M,)), dma((M,)),
        dma((D,)), dma((D,)), dma((M,)), dma((M,)), dma((D,)), dma((D,)), dma((M,)), dma((M,)),
        dma((5, M)), dma((5, M)), dma((6 + M,)), dma((6 + M,)),
    ]
    if G > 1:
        scratch += [
            pltpu.VMEM((G, M, U, K // 8), BF16),
            pltpu.VMEM((G, LP // 8, M * LP), BF16),
            dma((G, M)), dma((G, M)), dma((G,)), dma((G,)),
        ]
    out, gw1, gw2, vec = pl.pallas_call(
        functools.partial(kernel, D, M, U, LP, K, R),
        out_shape=[
            jax.ShapeDtypeStruct((U, R), BF16),
            jax.ShapeDtypeStruct((U, K), BF16),
            jax.ShapeDtypeStruct((U, -(-M * U // 128) * 128), BF16),
            jax.ShapeDtypeStruct((8, LP), F32),
        ],
        in_specs=[vmem] * 4 + [hbm] * 3,
        out_specs=[hbm, hbm, hbm, vmem],
        scratch_shapes=scratch,
        compiler_params=pltpu.CompilerParams(
            collective_id=0, has_side_effects=True, vmem_limit_bytes=64 * 2**20 - 2**18
        ),
    )(ids[None, :], hash_mult[None, :], hash_add[None, :], par, w1, w2p, cot)
    v = vec[:, :U]
    return (out, gw1.astype(F32), v[0], v[1], v[2], gw2[:, : M * U].astype(F32), v[3], v[4], v[5])


def solution(mesh):
    return jax.shard_map(
        per_device,
        mesh=mesh,
        in_specs=(
            P("dp"), P(), P(), P("mp", None), P("mp"), P("mp"), P("mp"),
            P("mp", None), P("mp"), P("mp"), P("mp"), P("mp", "dp"),
        ),
        out_specs=(
            P("mp", "dp"), P("mp", None), P("mp"), P("mp"), P("mp"),
            P("mp", None), P("mp"), P("mp"), P("mp"),
        ),
        check_vma=False,
    )
```

time: 868 us -> 275 us (0.32); the launches traced: 858 us -> 274 us
  waiting for transfers between devices: 494 us -> 0 us
  Pallas kernels: 0 us -> 259 us
  blocking collectives: 156 us -> 0 us
  matrix products: 91.3 us -> 0 us
  other arithmetic: 61.2 us -> 5.08 us
  local copies, waits for them, and re-layouts: 41 us -> 9.49 us
  between operations: 14.1 us -> 0.75 us
    all_gather x2 -> x0, waiting for transfers between devices: 442 us -> none  [the longest x1 254 us: per_device(): piece = lax.all_gather(d_pre_second, 'mp', axis=0, tiled=True)]
    pallas_call x0 -> x1, Pallas kernels: none -> 259 us  [per_device(): pl.pallas_call(functools.partial(kernel, D, M, U, LP, K, R), out_shape=[j...]
    all_to_all x1 -> x0, blocking collectives: 93.6 us -> none  [per_device(): lax.all_to_all(weight_second, 'mp', split_axis=1, concat_axis=0, tiled=True)]
    dot_general x5 -> x0, matrix products: 91.3 us -> none  [the longest x1 20.6 us: per_device(): lax.dot_general(hidden, piece, (((1,), (1,)), ((), ())), preferred_elemen...]
    psum x5 -> x0, blocking collectives: 62.6 us -> none  [the longest x1 14 us: per_device(): lax.psum(local_bias_first.astype(jnp.bfloat16), 'dp').astype(jnp.float32)]
    psum x1 -> x0, waiting for transfers between devices: 51.6 us -> none  [per_device(): lax.psum(local_weight_first.astype(jnp.bfloat16), 'dp').astype(jnp.float32)]
    reduce_sum x4 -> x0, other arithmetic: 43.7 us -> none  [the longest x1 14.2 us: per_device(): grad_bias_second = jnp.sum(d_pre_second.astype(jnp.float32), 1)]
    unnamed x38 -> x17, local copies, waits for them, and re-layouts: 29.7 us -> 1.9 us
  transfers between devices with their start and end apart: 3 -> 0, of which waited for: 3 -> 0; matrix products, arithmetic and copies ran while one was open for 1% -> 0% of each run, Pallas kernels for 0% -> 0%
where the time goes in v1:
time: 275 us; the launch traced here: 274 us
  Pallas kernels  259 us (94%)
  local copies, waits for them, and re-layouts  9.49 us (3%)
  other arithmetic  5.08 us (2%)
    pallas_call x1, Pallas kernels, per_device(): pl.pallas_call(functools.partial(kernel, D, M, U, LP, K, R), out_shape=[j...  259 us

profile of v1, /device:TPU:9, one launch (start us, length us, event | category | flops | bytes accessed | tf_op | source)
XLA Modules:
  0.0 274.4 jit_solution(7433317741969887782)
XLA Ops:
  0.6 2.2 fusion
  2.9 0.0 copy-start.2
  2.9 0.0 copy-start.3
  2.9 0.0 copy-start.4
  2.9 0.0 copy-start.5
  2.9 0.0 copy-start.6
  2.9 0.0 copy-start.7
  2.9 3.2 %concatenate.3.w2_ref = bf16[450,2048]{1,0:T(8,128)(2,1)} concatenate(bf16[450,450]{1,0:T(8,128)(2,1)S(1)} %get-tuple-element.19, bf16[450,62]{1,0:T(8,128)(2,1)S(1)} %broadcast_in_dim.15, bf16[450,450]{1,0:T(8,128)(2,1)S(1)} %get-tuple-element.18, bf16[450,62]{1,0:T(8,128)(2,1)S(1)} %broadcast_in_dim.15, bf16[450,450]{1,0:T(8,128)(2,1)S(1)} %get-tuple-element.20, ...), dimensions={1} | concatenate | bytes 3686400 | tf_op jit(solution)/shard_map/concatenate | solution.py:691
  6.1 0.0 copy-done.2
  6.1 0.0 copy-done.3
  6.1 0.0 copy-done.4
  6.1 0.0 copy-done.5
  6.1 0.0 copy-done.6
  6.2 0.0 copy-done.7
  6.2 0.6 pad.4.par_ref
  6.8 259.1 %shard_map.187 = (bf16[450,4096]{1,0:T(8,128)(2,1)}, bf16[450,1024]{1,0:T(8,128)(2,1)}, bf16[450,1920]{1,0:T(8,128)(2,1)}, f32[8,512]{1,0:T(8,128)}) custom-call(s32[1,4096]{1,0:T(1,128)} %bitcast.15, s32[1,1024]{1,0:T(1,128)} %bitcast.16, s32[1,1024]{1,0:T(1,128)} %bitcast.17, f32[8,512]{1,0:T(8,128)} %pad.4.par_ref, bf16[450,1024]{1,0:T(8,128)(2,1)} %w1_ref.1, ...), custom_call_target="tpu_custom_call" | custom-call | tf_op jit(solution)/shard_map/pallas_call | solution.py:733
  265.9 1.5 fusion.1
  267.4 0.0 copy-start.1
  267.4 0.0 copy-start
  267.5 3.6 %slice_convert_fusion = f32[450,1800]{1,0:T(8,128)} fusion(bf16[450,1920]{1,0:T(8,128)(2,1)} %get-tuple-element.16), kind=kLoop, calls=%fused_computation | loop fusion | flops 810000 | bytes 4860000 | tf_op jit(solution)/shard_map/convert_element_type | solution.py:749
  271.1 0.0 copy-done.1
  271.1 1.5 convert_element_type.8
  272.5 0.0 copy-done
  272.5 1.9 copy.22
  (2 shorter events, 0.1 us)
Async XLA Ops:
  2.9 3.3 %copy-start.2 = (f32[450]{0:T(512)S(1)}, f32[450]{0:T(512)}, u32[]{:S(2)}) copy-start(f32[450]{0:T(512)} %param.16) | copy-start | bytes 5404
  2.9 3.2 %copy-start.3 = (f32[450]{0:T(512)S(1)}, f32[450]{0:T(512)}, u32[]{:S(2)}) copy-start(f32[450]{0:T(512)} %param.17) | copy-start | bytes 5404
  2.9 3.2 %copy-start.4 = (f32[450]{0:T(512)S(1)}, f32[450]{0:T(512)}, u32[]{:S(2)}) copy-start(f32[450]{0:T(512)} %param.18) | copy-start | bytes 5404
  2.9 3.2 %copy-start.5 = (f32[450]{0:T(512)S(1)}, f32[450]{0:T(512)}, u32[]{:S(2)}) copy-start(f32[450]{0:T(512)} %param.20) | copy-start | bytes 5404
  2.9 3.2 %copy-start.6 = (f32[450]{0:T(512)S(1)}, f32[450]{0:T(512)}, u32[]{:S(2)}) copy-start(f32[450]{0:T(512)} %param.21) | copy-start | bytes 5404
  2.9 3.2 %copy-start.7 = (f32[450]{0:T(512)S(1)}, f32[450]{0:T(512)}, u32[]{:S(2)}) copy-start(f32[450]{0:T(512)} %param.22) | copy-start | bytes 5404
  267.4 3.6 %copy-start.1 = (bf16[450,1024]{1,0:T(8,128)(2,1)S(1)}, bf16[450,1024]{1,0:T(8,128)(2,1)}, u32[]{:S(2)}) copy-start(bf16[450,1024]{1,0:T(8,128)(2,1)} %get-tuple-element.14) | copy-start | bytes 2764804
  267.4 5.1 %copy-start = (bf16[450,4096]{1,0:T(8,128)(2,1)S(1)}, bf16[450,4096]{1,0:T(8,128)(2,1)}, u32[]{:S(2)}) copy-start(bf16[450,4096]{1,0:T(8,128)(2,1)} %get-tuple-element.36) | copy-start | bytes 11059204

commit v2 on v1

--- a/solution.py
+++ b/solution.py
@@ -54,7 +54,7 @@
     pv, ar1, ar2, ar2z, ar3, ar3z, ar4, ar4s, ar4z,
     w1s, w1r, w2s, w2r, pvs, pvr, cts, ctr, loc,
     a1s, a1r, a2s, a2r, a2zs, a2zr, a3s, a3r, a3zs, a3zr, a4s, a4r, a4zs, a4zr,
-    g1s, g1r, g2s, g2r, *extra,
+    g1s, g1r, g2s, g2r, free, *extra,
 ):
     Q = R // M
     G = D // 8
@@ -115,11 +115,12 @@
 
     w1_loc = pltpu.make_async_copy(w1_ref, C.at[m], loc.at[0])
     w1_loc.start()
-    w2_loc = pltpu.make_async_copy(w2_ref, W2.at[m], loc.at[1])
-    w2_loc.start()
     cot_loc = pltpu.make_async_copy(lanes(cot_ref, m * Q, Q), lanes(F.at[m], 0, Q), loc.at[2])
     cot_loc.start()
     pv[m] = par_ref[...]
+    for b in range(M):
+        W2[m, :, (b + 1) * LP - 128 : (b + 1) * LP] = jnp.zeros((U, 128), BF16)
+        W2[m, :, b * LP : b * LP + U] = w2_ref[:, b * U : (b + 1) * U]
     pl.semaphore_wait(bar, D - 1 + M - 1)
 
     ag1, ag2, agp, ct = {}, {}, {}, {}
@@ -131,10 +132,8 @@
         )
     for k in range(1, M):
         ag2[0, k] = send(
-            lanes(w2_ref, p * J8, J8), lanes(W2.at[m], p * J8, J8), w2s.at[0, k], w2r.at[0, k], (d, up[k])
+            lanes(W2.at[m], p * J8, J8), lanes(W2.at[m], p * J8, J8), w2s.at[0, k], w2r.at[0, k], (d, up[k])
         )
-    for k in range(1, M):
-        ct[k] = send(lanes(cot_ref, up[k] * Q, Q), lanes(F.at[m], 0, Q), cts.at[k], ctr.at[k], (d, up[k]))
 
     def gather_stage(step, ag, buf, size, ss, rs):
         dev, at, width = {
@@ -160,7 +159,7 @@
 
     HT = 128
 
-    def encode(q, slot):
+    def encode(q, put):
         def step(t, _):
             at = pl.multiple_of(t * HT, HT)
             both = hcol[pl.ds(at, HT), :].astype(I32)
@@ -169,17 +168,29 @@
                 top = lax.shift_right_logical(v, 16)
                 v = (v & 65535) + ((top << 4) - top)
             v = jnp.where(v >= 65521, v - 65521, v)
-            A[slot, pl.ds(at, HT), :] = (v.astype(F32) * (2.0 / 65520.0) - 1.0).astype(BF16)
+            put(t, (v.astype(F32) * (2.0 / 65520.0) - 1.0).astype(BF16))
             return 0
 
         lax.fori_loop(0, K // HT, step, 0)
+
+    def make_col(b):
+        col[b] = jnp.concatenate([RW[b], jnp.zeros((128 - RW.shape[1], LP), F32)], axis=0).T
 
     def make_cols():
         def step(b, _):
-            col[b] = jnp.concatenate([RW[b], jnp.zeros((128 - RW.shape[1], LP), F32)], axis=0).T
+            make_col(b)
             return 0
 
         lax.fori_loop(0, M, step, 0)
+
+    def to_a(q):
+        def put(t, value):
+            A[q, pl.ds(pl.multiple_of(t * HT, HT), HT), :] = value
+
+        return put
+
+    def to_e1(t, value):
+        E1[pl.ds(pl.multiple_of(lax.rem(t, LP // HT) * HT, HT), HT), pl.ds(pl.multiple_of(t // (LP // HT) * Q, 128), Q)] = value
 
     def row_of(slot):
         return jnp.sum(acc[slot].T, axis=0, keepdims=True)
@@ -188,23 +199,10 @@
     for b in range(M):
         B[pl.ds(b * LP + U // 16 * 16, LP - U // 16 * 16), :] = jnp.zeros((LP - U // 16 * 16, R), BF16)
 
-    encode(m, m)
-    encode(down[1], down[1])
-    stage1(1)
-
-    def enc_step(k, _):
-        q = lax.rem(m + M - k, M)
-        encode(q, q)
-        return 0
-
-    lax.fori_loop(2, M, enc_step, 0)
-    stage1(2)
-    for k in range(1, M):
-        agp[k].wait_recv()
-    for b in range(M):
-        RW[b, 0:8] = pv[b]
-        RW[b, 8:32] = jnp.zeros((24, LP), F32)
-    make_cols()
+    RW[...] = jnp.zeros_like(RW)
+    RW[m, 0:8] = par_ref[...]
+    make_col(m)
+    encode(m, to_a(m))
     w1_loc.wait()
 
     def mm1_own(b):
@@ -232,23 +230,39 @@
 
         lax.fori_loop(0, (M - 1) * NT, step, 0)
 
-    def mm1(b):
-        mm1_own(b)
-        mm1_rest(b)
+    def mm1_sums(b):
         ar1[d, pl.ds(b, 1), :] = row_of(0)
         ar1[d, pl.ds(b + M, 1), :] = row_of(1)
         acc[0:2] = jnp.zeros((2, LP, 128), F32)
 
-    mm1(m)
+    mm1_own(m)
+    stage1(1)
+
+    def enc_step(k, _):
+        q = lax.rem(m + M - k, M)
+        encode(q, to_a(q))
+        return 0
+
+    lax.fori_loop(1, M, enc_step, 0)
+    stage1(2)
+    mm1_rest(m)
+    mm1_sums(m)
+    stage1(3)
     stage2(1)
-    stage1(3)
+    for k in range(1, M):
+        ct[k] = send(lanes(cot_ref, up[k] * Q, Q), lanes(F.at[m], 0, Q), cts.at[k], ctr.at[k], (d, up[k]))
+    for k in range(1, M):
+        agp[k].wait_recv()
+    for b in range(M):
+        RW[b, 0:8] = pv[b]
+    make_cols()
     for k in range(1, M):
         ag1[3, k].wait_recv()
-        mm1(down[k])
+        mm1_own(down[k])
+        mm1_rest(down[k])
+        mm1_sums(down[k])
         if k == 1:
             stage2(2)
-        if k == 2:
-            stage2(3)
 
     def all_dp(buf, ss, rs):
         cps = []
@@ -265,6 +279,7 @@
         return out
 
     cps1 = all_dp(ar1, a1s, a1r)
+    stage2(3)
     for step in range(1, 4):
         for k in range(1, M):
             gone(ag1[step, k])
@@ -273,7 +288,6 @@
         cp = pltpu.make_async_copy(lanes(cot_ref, q * Q, Q), lanes(C.at[q], 0, Q), loc.at[3 + q])
         cot_all.append(cp)
         cp.start()
-    w2_loc.wait()
     for k in range(1, M):
         ag2[3, k].wait_recv()
 
@@ -369,12 +383,8 @@
     ar2z[m, 6:7] = sum_gn
     ar2z[m, 7:8] = jnp.zeros((1, LP), F32)
     cps2z = [send(ar2z.at[m], ar2z.at[m], a2zs.at[k], a2zr.at[k], (d, up[k])) for k in range(1, M)]
-    lax.fori_loop(2, M, own_loop, 0)
-    for cp in cps2z:
-        cp.wait_recv()
-    for b in range(M):
-        RW[b, 16:24] = ar2z[b]
-    make_cols()
+    RW[m, 16:24] = ar2z[m]
+    make_col(m)
 
     def back2(t, _):
         at = pl.multiple_of(t * TL, TL)
@@ -395,102 +405,137 @@
     ar3[d, 2 * M + 1 : 2 * M + 8, :] = jnp.zeros((7, LP), F32)
     acc[0:1] = jnp.zeros((1, LP, 128), F32)
 
-    PADAT = U // 16 * 16
-
-    def put_grad(b, value, at, size):
-        slot, row = a_at(NA, b)
-        A[slot, pl.ds(row, U), pl.ds(at, size)] = value
-
-    for b in range(M):
-        slot, row = NA + b // PER, (b % PER) * LP
-        A[slot, row + PADAT : row + LP, :] = jnp.where(
-            lax.broadcasted_iota(I32, (LP - PADAT, Q), 0) < U - PADAT,
-            A[slot, row + PADAT : row + LP, :].astype(F32),
+    L1 = pl.multiple_of(lax.rem(m + 1, M) * Q, 128)
+    LR = pl.multiple_of(L1 + LP, 128)
+
+    def rowsum(x):
+        acc[0, :U] = lane_part(x[:, : U // 128 * 128]) + jnp.where(
+            lax.broadcasted_iota(I32, (U, 128), 1) >= 128 - U % 128, x[:, U - 128 :], 0.0
+        )
+        return row_of(0)
+
+    def grad_w2(b, _):
+        at = pl.multiple_of(b * LP, LP)
+        g = dot_nt(B[pl.ds(at, LP), :], slo2[...])
+        w = W2[b, :, pl.ds(pl.multiple_of(m * LP, LP), LP)].astype(F32)[:, :U]
+        ar3[d, pl.ds(b, 1), :] = rowsum(w * gb2[:, :U])
+        ar3[d, pl.ds(b + M, 1), :] = rowsum(w * g[:U])
+        g = g * col[b, :, 1:2] + col[b, :, 2:3] * gb2[:, :U]
+        B[pl.ds(at, LP), pl.ds(L1, U)] = g.astype(BF16)
+        B[pl.ds(at, LP), pl.ds(L1 + U // 128 * 128, LP - U // 128 * 128)] = jnp.where(
+            lax.broadcasted_iota(I32, (LP, LP - U // 128 * 128), 1) < U - U // 128 * 128,
+            B[pl.ds(at, LP), pl.ds(L1 + U // 128 * 128, LP - U // 128 * 128)].astype(F32),
             0.0,
         ).astype(BF16)
-    cot_loc.wait()
-
-    def back2_own(b):
-        act_at, row = a_at(0, b)
-
-        def step(t, _):
-            at = pl.multiple_of(t * TL, TL)
-            a = A[act_at, pl.ds(row, U), pl.ds(at, TL)].astype(F32)
-            s = A[act_at + NA, pl.ds(row, U), pl.ds(at, TL)].astype(F32)
-            g = F[b, :, pl.ds(at, TL)].astype(F32)
-            grad = (g * col[b, :U, 16:17] + a * col[b, :U, 17:18] + col[b, :U, 18:19]) * s
-            A[act_at + NA, pl.ds(row, U), pl.ds(at, TL)] = grad.astype(BF16)
-            return 0
-
-        lax.fori_loop(0, NT, step, 0)
-
-    def copy_own(t, _):
-        at = pl.multiple_of(t * TL, TL)
-        put_grad(m, slo2[:, pl.ds(pl.multiple_of(m * Q + t * TL, TL), TL)], at, TL)
         return 0
 
-    lax.fori_loop(0, NT, copy_own, 0)
-    for k in range(1, M):
-        ct[k].wait_recv()
-        back2_own(down[k])
-
-    def d_hidden(b):
-        def step(t, _):
-            at = pl.multiple_of(t * TL, TL)
-            dh = dot(W2[b, :, 0:K], A[NA, :, pl.ds(at, TL)])
-            for n in range(1, NA):
-                dh = dh + dot(W2[b, :, n * K : (n + 1) * K], A[NA + n, :, pl.ds(at, TL)])
-            norm = B[pl.ds(pl.multiple_of(b * LP, LP), U), pl.ds(pl.multiple_of(m * Q + t * TL, TL), TL)].astype(F32)
-            F[b, :, pl.ds(at, TL)] = dh.astype(BF16)
-            acc[0, :U] += lane_part(dh)
-            acc[1, :U] += lane_part(dh * norm)
-            return 0
-
-        lax.fori_loop(0, NT, step, 0)
-        ar3[d, pl.ds(b, 1), :] = row_of(0)
-        ar3[d, pl.ds(b + M, 1), :] = row_of(1)
-        acc[0:2] = jnp.zeros((2, LP, 128), F32)
-
-    def d_hidden_step(b, _):
-        d_hidden(b)
-        return 0
-
-    lax.fori_loop(0, M, d_hidden_step, 0)
-    for step in range(1, 4):
+    lax.fori_loop(0, M, grad_w2, 0)
+    cps3 = all_dp(ar3, a3s, a3r)
+    for n, dev in ((0, core_dev), (1, hi_dev), (2, lo_dev)):
+        pl.semaphore_signal(free.at[n], inc=1, device_id=dev, device_id_type=MESH)
+    for k in range(1, M):
+        pl.semaphore_signal(free.at[2 + k], inc=1, device_id=(d, up[k]), device_id_type=MESH)
+
+    HALF = {0: (1 - c) * 4, 1: 4 * c + 2 * (1 - hi), 2: 4 * c + 2 * hi + 1 - lo}
+    KEEP = {0: 4 * c, 1: 4 * c + 2 * hi, 2: p}
+    START = {0: 0, 1: 4, 2: 6}
+    PARTNER = {0: core_dev, 1: hi_dev, 2: lo_dev}
+    g2cp = {}
+
+    def b_rows(b, at, size, lane):
+        return B.at[pl.ds(pl.multiple_of(b * LP + at * S8, 16), size * S8), pl.ds(lane, LP)]
+
+    def g2_send(n):
+        pl.semaphore_wait(free.at[n], 1)
+        for b in range(M):
+            g2cp[n, b] = send(
+                b_rows(b, HALF[n], 4 >> n, L1), b_rows(b, START[n], 4 >> n, LR), g2s.at[n, b], g2r.at[n, b], PARTNER[n]
+            )
+
+    def g2_add(n):
+        for b in range(M):
+            g2cp[n, b].wait_recv()
+            size = (4 >> n) * S8
+            keep = pl.ds(pl.multiple_of(b * LP + KEEP[n] * S8, 16), size)
+            came = pl.ds(b * LP + START[n] * S8, size)
+            B[keep, pl.ds(L1, LP)] = (
+                B[keep, pl.ds(L1, LP)].astype(F32) + B[came, pl.ds(LR, LP)].astype(F32)
+            ).astype(BF16)
+
+    def l2_of(z):
+        return pl.multiple_of(lax.rem(z + 2, M) * Q, 128)
+
+    L2 = l2_of(m)
+
+    if G > 1:
+        x1, x2, x1s, x1r, x2s, x2r = extra
+
+    def g2_groups():
+        cps = []
+        for k in range(1, G):
+            to = (lax.rem(d + 8 * k, D), m)
+            for b in range(M):
+                cps.append(send(b_rows(b, p, 1, L1), x2.at[d // 8, b], x2s.at[k, b], x2r.at[k, b], to))
+        for b in range(M):
+            x2[d // 8, b] = B[pl.ds(pl.multiple_of(b * LP + p * S8, 16), S8), pl.ds(L1, LP)]
+        for cp in cps:
+            cp.wait_recv()
+        for cp in cps:
+            gone(cp)
+        for b in range(M):
+            v = x2[0, b].astype(F32)
+            for k in range(1, G):
+                v = v + x2[k, b].astype(F32)
+            B[pl.ds(pl.multiple_of(b * LP + p * S8, 16), S8), pl.ds(L1, LP)] = v.astype(BF16)
+
+    def g2_z():
+        if G > 1:
+            g2_groups()
         for k in range(1, M):
-            gone(ag2[step, k])
-    cps3 = all_dp(ar3, a3s, a3r)
-
-    def grad_w2(b, _):
-        g = dot_nt(B[pl.ds(pl.multiple_of(b * LP, LP), LP), :], slo2[...])
-        g = g * col[b, :, 1:2] + col[b, :, 2:3] * gb2[:, :U]
-        E1[:, pl.ds(pl.multiple_of(b * LP, LP), U)] = g.astype(BF16)
-        return 0
-
-    lax.fori_loop(0, M, grad_w2, 0)
+            pl.semaphore_wait(free.at[2 + M - k], 1)
+            g2cp[3, k] = send(
+                b_rows(up[k], p, 1, L1),
+                B.at[pl.ds(pl.multiple_of(m * LP + p * S8, 16), S8), pl.ds(l2_of(up[k]), LP)],
+                g2s.at[3, k], g2r.at[3, k], (d, up[k]),
+            )
+        mine = pl.ds(pl.multiple_of(m * LP + p * S8, 16), S8)
+        B[mine, pl.ds(L2, LP)] = B[mine, pl.ds(L1, LP)]
+
+    def g2_gather(n):
+        at, size, dev = {4: (p, 1, lo_dev), 5: (4 * c + 2 * hi, 2, hi_dev), 6: (4 * c, 4, core_dev)}[n]
+        if n == 4:
+            for k in range(1, M):
+                g2cp[3, k].wait_recv()
+        else:
+            for b in range(M):
+                g2cp[n - 1, b].wait_recv()
+        for b in range(M):
+            part = b_rows(b, at, size, L2)
+            g2cp[n, b] = send(part, part, g2s.at[n, b], g2r.at[n, b], dev)
+
+    g2_send(0)
+    lax.fori_loop(2, M, own_loop, 0)
     tot = total(ar3, cps3)
     ar3z[m] = tot[: 2 * M]
     gb2_all = tot[2 * M : 2 * M + 1]
     cps3z = [send(ar3z.at[m], ar3z.at[m], a3zs.at[k], a3zr.at[k], (d, up[k])) for k in range(1, M)]
-    encode(m, 0)
+    g2_add(0)
+    g2_send(1)
+    encode(m, to_e1)
+    for cp in cps2z:
+        cp.wait_recv()
+    for b in range(M):
+        RW[b, 16:24] = ar2z[b]
     for cp in cps3z:
         cp.wait_recv()
     tot = ar3z[0]
     for b in range(1, M):
         tot = tot + ar3z[b]
-
-    R2 = W2.at[0]
-    h2 = LP // 2
-    g2cp = {}
-    g2cp[0] = send(rows(E1, (1 - c) * h2, h2), rows(R2, 0, h2), g2s.at[0], g2r.at[0], core_dev)
-
     for b in range(M):
         k1 = pv[b, 1:2] * RW[b, 9:10]
-        k2 = -k1 * tot[M + b : M + b + 1] / N
-        k3 = -k1 * tot[b : b + 1] / N
-        RW[b, 16:17] = k1
-        RW[b, 17:18] = k2
-        RW[b, 18:19] = k3
+        RW[b, 24:25] = k1
+        RW[b, 25:26] = -k1 * tot[M + b : M + b + 1] / N
+        RW[b, 26:27] = -k1 * tot[b : b + 1] / N
     make_cols()
     pick = lax.broadcasted_iota(I32, (2 * M, 1), 0)
     vec_ref[0:1, :] = jnp.zeros((1, LP), F32)
@@ -501,12 +546,56 @@
     vec_ref[5:6, :] = ar2z[m, 5:6]
     vec_ref[6:8, :] = jnp.zeros((2, LP), F32)
 
+    PADAT = U // 16 * 16
+
+    def put_grad(b, value, at, size):
+        slot, row = a_at(NA, b)
+        A[slot, pl.ds(row, U), pl.ds(at, size)] = value
+
+    for b in range(M):
+        slot, row = NA + b // PER, (b % PER) * LP
+        A[slot, row + PADAT : row + LP, :] = jnp.where(
+            lax.broadcasted_iota(I32, (LP - PADAT, Q), 0) < U - PADAT,
+            A[slot, row + PADAT : row + LP, :].astype(F32),
+            0.0,
+        ).astype(BF16)
+    cot_loc.wait()
+
+    def back2_own(b):
+        act_at, row = a_at(0, b)
+
+        def step(t, _):
+            at = pl.multiple_of(t * TL, TL)
+            a = A[act_at, pl.ds(row, U), pl.ds(at, TL)].astype(F32)
+            s = A[act_at + NA, pl.ds(row, U), pl.ds(at, TL)].astype(F32)
+            g = F[b, :, pl.ds(at, TL)].astype(F32)
+            grad = (g * col[b, :U, 16:17] + a * col[b, :U, 17:18] + col[b, :U, 18:19]) * s
+            A[act_at + NA, pl.ds(row, U), pl.ds(at, TL)] = grad.astype(BF16)
+            return 0
+
+        lax.fori_loop(0, NT, step, 0)
+
+    def copy_own(t, _):
+        at = pl.multiple_of(t * TL, TL)
+        put_grad(m, slo2[:, pl.ds(pl.multiple_of(m * Q + t * TL, TL), TL)], at, TL)
+        return 0
+
+    lax.fori_loop(0, NT, copy_own, 0)
+    for k in range(1, M):
+        ct[k].wait_recv()
+        back2_own(down[k])
+
+    g2_add(1)
+    g2_send(2)
+
     def back1(b):
         def step(t, _):
             at = pl.multiple_of(t * TL, TL)
+            dh = dot(W2[b, :, 0:K], A[NA, :, pl.ds(at, TL)])
+            for n in range(1, NA):
+                dh = dh + dot(W2[b, :, n * K : (n + 1) * K], A[NA + n, :, pl.ds(at, TL)])
             norm = B[pl.ds(pl.multiple_of(b * LP, LP), U), pl.ds(pl.multiple_of(m * Q + t * TL, TL), TL)].astype(F32)
-            dh = F[b, :, pl.ds(at, TL)].astype(F32)
-            grad = dh * col[b, :U, 16:17] + norm * col[b, :U, 17:18] + col[b, :U, 18:19]
+            grad = dh * col[b, :U, 24:25] + norm * col[b, :U, 25:26] + col[b, :U, 26:27]
             grad = (grad * H[b, :, pl.ds(at, TL)].astype(F32)).astype(BF16)
             H[b, :, pl.ds(at, TL)] = grad
             acc[0, :U] += lane_part(grad.astype(F32))
@@ -517,141 +606,111 @@
         acc[0:1] = jnp.zeros((1, LP, 128), F32)
 
         def mm(t, _):
-            at = pl.multiple_of(t * TL, TL)
-            F[b, :, pl.ds(at, TL)] = dot_nt(H[b], A[0, pl.ds(at, TL), :]).astype(BF16)
-            return 0
-
-        lax.fori_loop(0, K // TL, mm, 0)
-
-    ar4[d] = jnp.zeros((ar4.shape[1], LP), F32)
-    K4, K2, half = 2 * K8, 4 * K8, K // 2
-    g1cp = {}
-    for b in range(M):
-        back1(b)
-        g1cp[0, b] = send(
-            lanes(F.at[b], (1 - c) * K2, K2), lanes(C.at[b], 0, K2), g1s.at[0, b], g1r.at[0, b], core_dev
-        )
-    cps4 = all_dp(ar4, a4s, a4r)
-
-    def add_rows(to, at, other, size):
-        def step(t, _):
-            s = pl.multiple_of(t * 16, 16)
-            to[pl.ds(pl.multiple_of(at + s, 16), 16), :] = (
-                to[pl.ds(pl.multiple_of(at + s, 16), 16), :].astype(F32) + other(s).astype(F32)
+            F[b, :, pl.ds(pl.multiple_of(t * LP, LP), LP)] = dot_nt(
+                H[b], E1[:, pl.ds(pl.multiple_of(t * Q, Q), Q)]
             ).astype(BF16)
             return 0
 
-        lax.fori_loop(0, size // 16, step, 0)
-
-    def g2_step(n):
-        g2cp[n - 1].wait_recv()
-        size = h2 >> (n - 1)
-        at = {1: 4 * c, 2: 4 * c + 2 * hi, 3: p}[n] * S8
-        start = {1: 0, 2: h2, 3: h2 + h2 // 2}[n]
-        add_rows(E1, at, lambda s: W2[0, pl.ds(pl.multiple_of(start + s, 16), 16), :], size)
-
-    def g1_step(n, b):
-        g1cp[n - 1, b].wait_recv()
-        size = K2 >> (n - 1)
-        at = pl.multiple_of({1: 4 * c, 2: 4 * c + 2 * hi, 3: p}[n] * K8, 128)
-        start = {1: 0, 2: K2, 3: K2 + K4}[n]
-        F[b, :, pl.ds(at, size)] = (
-            F[b, :, pl.ds(at, size)].astype(F32) + C[b, :, start : start + size].astype(F32)
-        ).astype(BF16)
-
-    g2_step(1)
-    g2cp[1] = send(
-        rows(E1, (4 * c + 2 * (1 - hi)) * S8, 2 * S8), rows(R2, h2, 2 * S8), g2s.at[1], g2r.at[1], hi_dev
-    )
-    for b in range(M):
-        g1_step(1, b)
-        g1cp[1, b] = send(
-            lanes(F.at[b], (4 * c + 2 * (1 - hi)) * K8, K4), lanes(C.at[b], K2, K4), g1s.at[1, b], g1r.at[1, b], hi_dev
+        lax.fori_loop(0, PER, mm, 0)
+
+    acc[0:1] = jnp.zeros((1, LP, 128), F32)
+    ar4[d] = jnp.zeros((ar4.shape[1], LP), F32)
+    K2 = 4 * K8
+    FROM = {0: 0, 1: K2, 2: K2 + 2 * K8}
+    order = [up[(j + 1) % M] for j in range(M)]
+    g1cp = {}
+
+    def g1_send(n, j):
+        b = order[j]
+        g1cp[n, j] = send(
+            lanes(F.at[b], HALF[n] * K8, K2 >> n), lanes(C.at[b], FROM[n], K2 >> n), g1s.at[n, j], g1r.at[n, j], PARTNER[n]
         )
-    tot4 = total(ar4, cps4)
-    for b in range(M):
-        ar4s[b] = jnp.broadcast_to(tot4[b : b + 1], (8, LP))
-    ar4z[m] = ar4s[m]
-    cps4z = [send(ar4s.at[up[k]], ar4z.at[m], a4zs.at[k], a4zr.at[k], (d, up[k])) for k in range(1, M)]
-    g2_step(2)
-    g2cp[2] = send(
-        rows(E1, (4 * c + 2 * hi + 1 - lo) * S8, S8), rows(R2, h2 + 2 * S8, S8), g2s.at[2], g2r.at[2], lo_dev
-    )
-    for b in range(M):
-        g1_step(2, b)
-        g1cp[2, b] = send(
-            lanes(F.at[b], (4 * c + 2 * hi + 1 - lo) * K8, K8), lanes(C.at[b], K2 + K4, K8), g1s.at[2, b], g1r.at[2, b], lo_dev
-        )
-    g2_step(3)
-    for b in range(M):
-        g1_step(3, b)
-    if G > 1:
-        x1, x2, x1s, x1r, x2s, x2r = extra
-        cpsx = []
+
+    def g1_add(n, j):
+        b = order[j]
+        g1cp[n, j].wait_recv()
+        keep = pl.ds(pl.multiple_of(KEEP[n] * K8, 128), K2 >> n)
+        F[b, :, keep] = (F[b, :, keep].astype(F32) + C[b, :, FROM[n] : FROM[n] + (K2 >> n)].astype(F32)).astype(BF16)
+
+    def g1_groups(j):
+        b = order[j]
+        mine = pl.ds(pl.multiple_of(p * K8, 128), K8)
+        cps = []
         for k in range(1, G):
             to = (lax.rem(d + 8 * k, D), m)
-            cpsx.append(send(rows(E1, p * S8, S8), x2.at[d // 8], x2s.at[k], x2r.at[k], to))
+            cps.append(send(lanes(F.at[b], p * K8, K8), x1.at[d // 8, j], x1s.at[k, j], x1r.at[k, j], to))
+        x1[d // 8, j] = F[b, :, mine]
+        for cp in cps:
+            cp.wait_recv()
+        for cp in cps:
+            gone(cp)
+        v = x1[0, j].astype(F32)
+        for k in range(1, G):
+            v = v + x1[k, j].astype(F32)
+        F[b, :, mine] = v.astype(BF16)
+
+    def g1_z(j):
+        if G > 1:
+            g1_groups(j)
+        b, k = order[j], (j + 1) % M
+        if k:
+            g1cp[3, j] = send(
+                lanes(F.at[b], p * K8, K8), C.at[m, :, pl.ds(K - K8, K8)], g1s.at[3, k], g1r.at[3, k], (d, b)
+            )
+        else:
+            C[m, :, K - K8 : K] = F[m, :, pl.ds(pl.multiple_of(p * K8, 128), K8)]
+
+    def g1_stage(n, j):
+        if 0 <= j < M:
+            g1_add(n - 1, j)
+            if n < 3:
+                g1_send(n, j)
+            else:
+                g1_z(j)
+
+    for j in range(M + 3):
+        if j < M:
+            back1(order[j])
+            g1_send(0, j)
+        if j == M - 1:
+            cps4 = all_dp(ar4, a4s, a4r)
+        g1_stage(3, j - 3)
+        g1_stage(2, j - 2)
+        g1_stage(1, j - 1)
+        if j == 0:
+            g2_add(2)
+            g2_z()
+        if j == 1:
+            g2_gather(4)
+        if j == 2:
+            g2_gather(5)
+        if j == 3:
+            g2_gather(6)
+        if j == M:
+            tot4 = total(ar4, cps4)
             for b in range(M):
-                cpsx.append(send(lanes(F.at[b], p * K8, K8), x1.at[d // 8, b], x1s.at[k, b], x1r.at[k, b], to))
-        x2[d // 8] = E1[pl.ds(pl.multiple_of(p * S8, 16), S8), :]
-        for b in range(M):
-            x1[d // 8, b] = F[b, :, pl.ds(pl.multiple_of(p * K8, 128), K8)]
-        for cp in cpsx:
-            cp.wait()
-        v = x2[0].astype(F32)
-        for k in range(1, G):
-            v = v + x2[k].astype(F32)
-        E1[pl.ds(pl.multiple_of(p * S8, 16), S8), :] = v.astype(BF16)
-        for b in range(M):
-            v = x1[0, b].astype(F32)
-            for k in range(1, G):
-                v = v + x1[k, b].astype(F32)
-            F[b, :, pl.ds(pl.multiple_of(p * K8, 128), K8)] = v.astype(BF16)
-
-    g1z = [
-        send(
-            lanes(F.at[up[k]], p * K8, K8), C.at[m, :, pl.ds(K2 + K4 + K8, K8)], g1s.at[3, k], g1r.at[3, k], (d, up[k])
-        )
-        for k in range(1, M)
-    ]
-    Z2 = W2.at[1]
-    p64 = pl.multiple_of(p * S8, 16)
-    g2z = [
-        send(
-            E1.at[pl.ds(p64, S8), pl.ds(pl.multiple_of(up[k] * LP, LP), LP)],
-            Z2.at[pl.ds(0, S8), pl.ds(pl.multiple_of(m * LP, LP), LP)],
-            g2s.at[3 + k], g2r.at[3 + k], (d, up[k]),
-        )
-        for k in range(1, M)
-    ]
-    C[m, :, K2 + K4 + K8 : K] = F[m, :, pl.ds(pl.multiple_of(p * K8, 128), K8)]
-    W2[1, 0:S8, pl.ds(pl.multiple_of(m * LP, LP), LP)] = E1[
-        pl.ds(p64, S8), pl.ds(pl.multiple_of(m * LP, LP), LP)
-    ]
-    for cp in g1z:
-        cp.wait_recv()
-    v = C[0, :, K2 + K4 + K8 : K].astype(F32)
+                ar4s[b] = jnp.broadcast_to(tot4[b : b + 1], (8, LP))
+            ar4z[m] = ar4s[m]
+            cps4z = [send(ar4s.at[up[k]], ar4z.at[m], a4zs.at[k], a4zr.at[k], (d, up[k])) for k in range(1, M)]
+    for b in range(M):
+        g2cp[6, b].wait_recv()
+    for b in range(M):
+        slo2[:, b * U : (b + 1) * U] = B[b * LP : b * LP + U, pl.ds(L2, LP)][:, :U]
+    gw2_copy = pltpu.make_async_copy(lanes(slo2, 0, gw2_ref.shape[1]), gw2_ref, loc.at[2])
+    gw2_copy.start()
+    for j in range(M - 1):
+        g1cp[3, j].wait_recv()
+    v = C[0, :, K - K8 : K].astype(F32)
     for b in range(1, M):
-        v = v + C[b, :, K2 + K4 + K8 : K].astype(F32)
+        v = v + C[b, :, K - K8 : K].astype(F32)
     G1[:, pl.ds(pl.multiple_of(p * K8, 128), K8)] = v.astype(BF16)
     ga = send(lanes(G1, p * K8, K8), lanes(G1, p * K8, K8), g1s.at[4, 0], g1r.at[4, 0], lo_dev)
-    for cp in g2z:
-        cp.wait_recv()
-    at2 = pl.multiple_of((2 * hi + lo) * S8, 16)
-    W2[2 + c, pl.ds(at2, S8), :] = W2[1, 0:S8, :]
-    gb = send(rows(W2.at[2 + c], at2, S8), rows(W2.at[2 + c], at2, S8), g2s.at[3 + M], g2r.at[3 + M], lo_dev)
     ga.wait_recv()
-    part = lanes(G1, (4 * c + 2 * hi) * K8, K4)
+    part = lanes(G1, (4 * c + 2 * hi) * K8, 2 * K8)
     ga = send(part, part, g1s.at[4, 1], g1r.at[4, 1], hi_dev)
-    gb.wait_recv()
-    part = rows(W2.at[2 + c], 2 * hi * S8, 2 * S8)
-    gb = send(part, part, g2s.at[4 + M], g2r.at[4 + M], hi_dev)
     ga.wait_recv()
     part = lanes(G1, 4 * c * K8, K2)
     ga = send(part, part, g1s.at[4, 2], g1r.at[4, 2], core_dev)
-    gb.wait_recv()
-    part = rows(W2.at[2 + c], 0, 4 * S8)
-    gb = send(part, part, g2s.at[5 + M], g2r.at[5 + M], core_dev)
     for cp in cps4z:
         cp.wait_recv()
     v = ar4z[0]
@@ -661,14 +720,6 @@
     ga.wait_recv()
     gw1_copy = pltpu.make_async_copy(G1, gw1_ref, loc.at[1])
     gw1_copy.start()
-    gb.wait_recv()
-    top = min(4 * S8, U)
-    for b in range(M):
-        slo2[0:top, b * U : (b + 1) * U] = W2[2, 0:top, b * LP : b * LP + U]
-        if U > top:
-            slo2[top:U, b * U : (b + 1) * U] = W2[3, 0 : U - top, b * LP : b * LP + U]
-    gw2_copy = pltpu.make_async_copy(lanes(slo2, 0, gw2_ref.shape[1]), gw2_ref, loc.at[2])
-    gw2_copy.start()
     out_copy.wait()
     gw1_copy.wait()
     gw2_copy.wait()
@@ -684,11 +735,6 @@
     LP = -(-U // 128) * 128
     G = D // 8
     par = jnp.pad(jnp.stack([b1, s1, t1, b2, s2, t2]), ((0, 2), (0, LP - U)))
-    zeros = jnp.zeros((U, LP - U), BF16)
-    pieces = []
-    for b in range(M):
-        pieces += [w2[:, b * U : (b + 1) * U], zeros]
-    w2p = jnp.concatenate(pieces, axis=1)
     dma = pltpu.SemaphoreType.DMA
     vmem = pl.BlockSpec(memory_space=pltpu.VMEM)
     hbm = pl.BlockSpec(memory_space=pl.ANY)
@@ -722,13 +768,13 @@
         dma((M,)), dma((M,)), dma((M,)), dma((M,)), dma((3 + M,)),
         dma((D,)), dma((D,)), dma((D,)), dma((D,)), dma((M,)), dma((M,)),
         dma((D,)), dma((D,)), dma((M,)), dma((M,)), dma((D,)), dma((D,)), dma((M,)), dma((M,)),
-        dma((5, M)), dma((5, M)), dma((6 + M,)), dma((6 + M,)),
+        dma((5, M)), dma((5, M)), dma((7, M)), dma((7, M)), pltpu.SemaphoreType.REGULAR((2 + M,)),
     ]
     if G > 1:
         scratch += [
             pltpu.VMEM((G, M, U, K // 8), BF16),
-            pltpu.VMEM((G, LP // 8, M * LP), BF16),
-            dma((G, M)), dma((G, M)), dma((G,)), dma((G,)),
+            pltpu.VMEM((G, M, LP // 8, LP), BF16),
+            dma((G, M)), dma((G, M)), dma((G, M)), dma((G, M)),
         ]
     out, gw1, gw2, vec = pl.pallas_call(
         functools.partial(kernel, D, M, U, LP, K, R),
@@ -738,13 +784,13 @@
             jax.ShapeDtypeStruct((U, -(-M * U // 128) * 128), BF16),
             jax.ShapeDtypeStruct((8, LP), F32),
         ],
-        in_specs=[vmem] * 4 + [hbm] * 3,
+        in_specs=[vmem] * 4 + [hbm, vmem, hbm],
         out_specs=[hbm, hbm, hbm, vmem],
         scratch_shapes=scratch,
         compiler_params=pltpu.CompilerParams(
             collective_id=0, has_side_effects=True, vmem_limit_bytes=64 * 2**20 - 2**18
         ),
-    )(ids[None, :], hash_mult[None, :], hash_add[None, :], par, w1, w2p, cot)
+    )(ids[None, :], hash_mult[None, :], hash_add[None, :], par, w1, w2, cot)
     v = vec[:, :U]
     return (out, gw1.astype(F32), v[0], v[1], v[2], gw2[:, : M * U].astype(F32), v[3], v[4], v[5])
 

time: 275 us -> 218 us (0.79)
  Pallas kernels: 259 us -> 204 us
  local copies, waits for them, and re-layouts: 9.49 us -> 4.81 us
    pallas_call x1, Pallas kernels: 259 us -> 204 us  [per_device(): pl.pallas_call(functools.partial(kernel, D, M, U, LP, K, R), out_shape=[j...]
    concatenate x1 -> x0, local copies, waits for them, and re-layouts: 3.18 us -> none  [per_device(): w2p = jnp.concatenate(pieces, axis=1)]
where the time goes in v2:
time: 218 us; the launch traced here: 215 us
  Pallas kernels  204 us (94%)
  other arithmetic  5.08 us (2%)
  local copies, waits for them, and re-layouts  4.81 us (2%)
    pallas_call x1, Pallas kernels, per_device(): pl.pallas_call(functools.partial(kernel, D, M, U, LP, K, R), out_shape=[j...  204 us

profile of v2, /device:TPU:9, one launch (start us, length us, event | category | flops | bytes accessed | tf_op | source)
XLA Modules:
  0.0 215.0 jit_solution(13979230571925458196)
XLA Ops:
  0.6 0.8 stack.27
  1.4 0.6 pad.4.par_ref
  2.0 204.5 %shard_map.187 = (bf16[450,4096]{1,0:T(8,128)(2,1)}, bf16[450,1024]{1,0:T(8,128)(2,1)}, bf16[450,1920]{1,0:T(8,128)(2,1)}, f32[8,512]{1,0:T(8,128)}) custom-call(s32[1,4096]{1,0:T(1,128)} %bitcast.15, s32[1,1024]{1,0:T(1,128)} %bitcast.16, s32[1,1024]{1,0:T(1,128)} %bitcast.17, f32[8,512]{1,0:T(8,128)} %pad.4.par_ref, bf16[450,1024]{1,0:T(8,128)(2,1)} %w1_ref.1, ...), custom_call_target="tpu_custom_call" | custom-call | tf_op jit(solution)/shard_map/pallas_call | solution.py:779
  206.5 0.0 copy-start.1
  206.5 1.5 fusion
  208.1 0.0 copy-start
  208.1 3.6 %slice_convert_fusion = f32[450,1800]{1,0:T(8,128)} fusion(bf16[450,1920]{1,0:T(8,128)(2,1)} %get-tuple-element.16), kind=kLoop, calls=%fused_computation | loop fusion | flops 810000 | bytes 4860000 | tf_op jit(solution)/shard_map/convert_element_type | solution.py:795
  211.7 0.0 copy-done.1
  211.7 1.5 convert_element_type.8
  213.1 0.0 copy-done
  213.1 1.9 copy.22
Async XLA Ops:
  206.5 5.2 %copy-start.1 = (bf16[450,1024]{1,0:T(8,128)(2,1)S(1)}, bf16[450,1024]{1,0:T(8,128)(2,1)}, u32[]{:S(2)}) copy-start(bf16[450,1024]{1,0:T(8,128)(2,1)} %get-tuple-element.14) | copy-start | bytes 2764804
  208.1 5.1 %copy-start = (bf16[450,4096]{1,0:T(8,128)(2,1)S(1)}, bf16[450,4096]{1,0:T(8,128)(2,1)}, u32[]{:S(2)}) copy-start(bf16[450,4096]{1,0:T(8,128)(2,1)} %get-tuple-element.32) | copy-start | bytes 11059204
